TPU v7x, 32 devices: a whole 2x2x4 slice. The times are simulated.
32 devices in a mesh: seq: 4 (over z), head: 4 (over y, x), dp: 2 (over core).
Axes of the slice: x: 2, y: 2, z: 4, core: 2. Of those that a mesh axis runs over, the one named last changes fastest.
Arguments:
- queries: bfloat16 [2, 512, 4096], P('dp', 'seq', 'head'), may hold values from -0.23925781 to 0.23925781
- key_rows: bfloat16 [2, 512, 4096], P('dp', 'seq', 'head'), may hold values from -0.23925781 to 0.23925781
- values: bfloat16 [2, 512, 4096], P('dp', 'seq', 'head'), may hold values from -6 to 6
- out_grad: bfloat16 [2, 512, 4096], P('dp', 'seq', 'head'), may hold values from -6 to 6
- decay_rate: float32 [32], P('head'), may hold values from 4e-05 to 0.025, as said below
- rotation: float32 [4, 4096], P(None, 'head')
- refusal: float32 [4096, 2], P('head')
- proj_weight: float32 [4, 4096], P(None, 'head'), may hold values from -0.09375 to 0.09375
- proj_bias: float32 [4], replicated, may hold values from -4 to 4
- positions: int32 [2, 16], P('dp'), may hold values from 0 to 511, as said below
Outputs:
- attended: bfloat16 [2, 512, 4096], P('dp', 'seq', 'head')
- grad_query: bfloat16 [2, 512, 4096], P('dp', 'seq', 'head')
- grad_key: bfloat16 [2, 512, 4096], P('dp', 'seq', 'head')
- grad_value: bfloat16 [2, 512, 4096], P('dp', 'seq', 'head')
- grad_rotation: float32 [4, 4096], P(None, 'head')
- grad_weight: float32 [4, 4096], P(None, 'head')
- grad_bias: float32 [4], replicated
Inputs may be any that keep to these rules, and one draw needn't show every extreme that they name: 16 distinct positions in ascending order; among them always 0, 256 and 511. `decay_rate`: one rate per head, the same at every position.
All inputs are finite; a program needn't handle non-finite values.
Results may differ from a plain program's by a relative error of at most 0.0032.
Values sent between devices are 32-bit elements; how exact they have to be, the bound alone decides.
A program may use at most 128 MiB of HBM per device.

v0:
```python
import jax
import jax.numpy as jnp
from jax import lax
from jax.sharding import PartitionSpec as P

highest = lax.Precision.HIGHEST


def carried_in(x, axis, combine, identity, reverse):
    peers, place = (lax.axis_size(axis), lax.axis_index(axis))
    everything = jax.tree.map(lambda part: lax.all_gather(part, axis), x)
    start = jax.tree.map(
        lambda part, zero: jnp.broadcast_to(jnp.asarray(zero, part.dtype), part.shape), x, identity
    )

    def lap(k, before):
        at = peers - 1 - k if reverse else k
        reached = at > place if reverse else at < place
        new = combine(before, jax.tree.map(lambda part: part[at], everything))
        return jax.tree.map(lambda a, b: jnp.where(reached, a, b), new, before)

    return lax.fori_loop(0, peers, lap, start)


def decay_table(log_decay, count):
    offsets = jnp.arange(count)
    between = offsets[:, None] - offsets[None, :]
    powers = jnp.exp(jnp.maximum(between, 0).astype(jnp.float32)[None] * log_decay[:, None, None])
    return jnp.where(between[None] >= 0, powers, 0.0)


def gram_inverse(gram):
    determinant = gram[0, 0] * gram[1, 1] - gram[0, 1] * gram[1, 0]
    adjugate = jnp.stack(
        [jnp.stack([gram[1, 1], -gram[0, 1]]), jnp.stack([-gram[1, 0], gram[0, 0]])]
    )
    return adjugate / determinant


def chain_combine(earlier, later):
    return (earlier[0] * later[0], later[0][:, None, None] * earlier[1] + later[1])


def shards(
    queries,
    key_rows,
    values,
    out_grad,
    decay_rate,
    rotation,
    refusal,
    proj_weight,
    proj_bias,
    positions,
):
    group = queries.shape[1]
    local_width = queries.shape[2]
    local_heads = decay_rate.shape[0]
    head_size = local_width // local_heads
    query_heads = queries[0].reshape(group, local_heads, head_size)
    key_heads = key_rows[0].reshape(group, local_heads, head_size)
    grad_heads = out_grad[0].reshape(group, local_heads, head_size)
    places = lax.axis_index("seq") * group + jnp.arange(group, dtype=jnp.int32)
    selector = places[:, None] == positions[0][None, :]
    select_low = selector.astype(jnp.bfloat16)
    select_full = selector.astype(jnp.float32)
    picked = jnp.dot(select_low.T, values[0], preferred_element_type=jnp.float32)
    gram_part = jnp.dot(refusal.T, refusal, precision=highest)
    coupling_part = jnp.dot(rotation, refusal, precision=highest)
    gram, coupling = lax.psum((gram_part, coupling_part), "head")
    inverse = gram_inverse(gram)
    rotated = rotation - jnp.dot(
        jnp.dot(coupling, inverse, precision=highest), refusal.T, precision=highest
    )
    code = (
        lax.psum(jnp.dot(picked, (proj_weight - rotated).T, precision=highest), "head") + proj_bias
    )
    shift_rows = jnp.dot(code, rotated, precision=highest)
    moved = (
        values[0].astype(jnp.float32) + jnp.dot(select_full, shift_rows, precision=highest)
    ).astype(jnp.bfloat16)
    moved_heads = moved.reshape(group, local_heads, head_size)
    log_decay = jnp.log1p(-decay_rate)
    table = decay_table(log_decay, group)
    offsets = jnp.arange(group).astype(jnp.float32)
    enter = jnp.exp((offsets + 1.0)[:, None] * log_decay[None, :])
    leave = jnp.exp((group - offsets)[:, None] * log_decay[None, :])
    start_weight = jnp.exp(offsets[:, None] * log_decay[None, :])
    end_weight = jnp.exp((group - 1.0 - offsets)[:, None] * log_decay[None, :])
    keep = jnp.exp(group * log_decay)
    query_full = query_heads.astype(jnp.float32)
    key_full = key_heads.astype(jnp.float32)
    moved_full = moved_heads.astype(jnp.float32)
    grad_full = grad_heads.astype(jnp.float32)
    local_state = jnp.einsum(
        "shd,she->hde", key_full * end_weight[:, :, None], moved_full, precision=highest
    )
    local_grad = jnp.einsum(
        "thd,the->hde", query_full * start_weight[:, :, None], grad_full, precision=highest
    )
    blank = (jnp.ones_like(keep), jnp.zeros_like(local_state))
    entering = carried_in((keep, local_state), "seq", chain_combine, blank, False)[1]
    leaving = carried_in((keep, local_grad), "seq", chain_combine, blank, True)[1]
    scores = jnp.einsum("thd,shd->hts", query_heads, key_heads, preferred_element_type=jnp.float32)
    mixing = (scores * table).astype(jnp.bfloat16)
    inner = jnp.einsum("hts,she->the", mixing, moved_heads, preferred_element_type=jnp.float32)
    outer = enter[:, :, None] * jnp.einsum("thd,hde->the", query_full, entering, precision=highest)
    attended = (inner + outer).astype(jnp.bfloat16).reshape(1, group, local_width)
    grad_scores = jnp.einsum(
        "the,she->hts", grad_heads, moved_heads, preferred_element_type=jnp.float32
    )
    grad_mixing = (grad_scores * table).astype(jnp.bfloat16)
    grad_query = jnp.einsum(
        "hts,shd->thd", grad_mixing, key_heads, preferred_element_type=jnp.float32
    )
    grad_query = grad_query + enter[:, :, None] * jnp.einsum(
        "the,hde->thd", grad_full, entering, precision=highest
    )
    grad_key = jnp.einsum(
        "hts,thd->shd", grad_mixing, query_heads, preferred_element_type=jnp.float32
    )
    grad_key = grad_key + leave[:, :, None] * jnp.einsum(
        "she,hde->shd", moved_full, leaving, precision=highest
    )
    grad_moved = jnp.einsum("hts,the->she", mixing, grad_heads, preferred_element_type=jnp.float32)
    grad_moved = grad_moved + leave[:, :, None] * jnp.einsum(
        "shd,hde->she", key_full, leaving, precision=highest
    )
    grad_moved = grad_moved.reshape(group, local_width)
    picked_grad = jnp.dot(select_full.T, grad_moved, precision=highest)
    code_grad = lax.psum(jnp.dot(picked_grad, rotated.T, precision=highest), "head")
    rotated_grad = jnp.dot(code.T, picked_grad, precision=highest) - jnp.dot(
        code_grad.T, picked, precision=highest
    )
    projected = lax.psum(jnp.dot(rotated_grad, refusal, precision=highest), "head")
    rotation_part = rotated_grad - jnp.dot(
        jnp.dot(projected, inverse, precision=highest), refusal.T, precision=highest
    )
    weight_part = jnp.dot(code_grad.T, picked, precision=highest)
    bias_part = jnp.sum(code_grad, axis=0)
    grad_weight, grad_bias, grad_rotation = lax.psum(
        (weight_part, bias_part, rotation_part), ("seq", "dp")
    )
    value_fix = jnp.dot(code_grad, proj_weight - rotated, precision=highest)
    grad_value = (
        (grad_moved + jnp.dot(select_full, value_fix, precision=highest))
        .astype(jnp.bfloat16)
        .reshape(1, group, local_width)
    )
    grad_query = grad_query.astype(jnp.bfloat16).reshape(1, group, local_width)
    grad_key = grad_key.astype(jnp.bfloat16).reshape(1, group, local_width)
    return (attended, grad_query, grad_key, grad_value, grad_rotation, grad_weight, grad_bias)


def solution(mesh):
    return jax.shard_map(
        shards,
        mesh=mesh,
        in_specs=(
            P("dp", "seq", "head"),
            P("dp", "seq", "head"),
            P("dp", "seq", "head"),
            P("dp", "seq", "head"),
            P("head"),
            P(None, "head"),
            P("head", None),
            P(None, "head"),
            P(),
            P("dp", None),
        ),
        out_specs=(
            P("dp", "seq", "head"),
            P("dp", "seq", "head"),
            P("dp", "seq", "head"),
            P("dp", "seq", "head"),
            P(None, "head"),
            P(None, "head"),
            P(),
        ),
        check_vma=False,
    )
```

profile of v0, /device:TPU:0, one launch (start us, length us, event | category | flops | bytes accessed | tf_op | source)
XLA Modules:
  0.0 145.7 jit_solution(9627243468907765891)
XLA Ops:
  7.3 1.2 copy.66
  8.5 1.1 copy.67
  9.7 1.2 dynamic-slice
  11.6 0.8 negate_log-plus-one_fusion
  12.4 1.5 %fusion.20 = f32[8,128,128]{2,1,0:T(8,128)} fusion(bf16[128,8,128]{0,2,1:T(8,128)(2,1)S(1)} %bitcast.150, bf16[128,8,128]{0,2,1:T(8,128)(2,1)S(1)} %bitcast.146, f32[128,8]{0,1:T(8,128)S(1)} %get-tuple-element.318), kind=kOutput, calls=%fused_computation.39 | convolution fusion | flops 201588736 | bytes 1052672 | tf_op jit(solution)/shard_map/thd,the->hde/dot_general | solution.py:98
  14.3 11.4 %all-reduce.3 = (f32[4,2]{1,0:T(4,128)S(1)}, f32[2,2]{1,0:T(2,128)S(1)}) all-reduce(f32[4,2]{1,0:T(4,128)S(1)} %fusion.63, f32[2,2]{1,0:T(2,128)S(1)} %fusion.64), channel_id=1, replica_groups=mesh['seq'=4,'head'=4,'dp'=2] {'head'}, use_global_device_ids=true, to_apply=%region_0.0 | all-reduce | flops 12 | bytes 96 | tf_op jit(solution)/shard_map/psum | solution.py:70
  25.7 0.6 fusion.62
  28.8 12.2 %all-reduce = f32[32]{0:T(128)S(1)} all-reduce(f32[32]{0:T(128)S(1)} %get-tuple-element.321), channel_id=2, replica_groups=mesh['seq'=4,'head'=4,'dp'=2] {'seq'}, use_global_device_ids=true, to_apply=%add | all-reduce | flops 32 | bytes 256
  41.0 0.7 reshape.193
  43.3 1.4 maximum_bitcast_fusion
  45.5 0.4 fusion.13
  45.9 17.0 %all-gather.8.cloned.1.call-done = f32[32,128,128]{2,1,0:T(8,128)} async-done(((f32[8,128,128]{2,1,0:T(8,128)}), f32[32,128,128]{2,1,0:T(8,128)}) %all-gather.8.cloned.1.call-update) | async-done | bytes 2097168 | tf_op jit(solution)/shard_map/all_gather | solution.py:11
  62.9 7.5 %while.31 = (s32[]{:T(128)}, f32[8,128,128]{2,1,0:T(8,128)S(1)}, s32[]{:T(128)}, f32[4,8]{1,0:T(4,128)}, f32[4,8,128,128]{3,2,1,0:T(8,128)}, /*index=5*/s32[]{:T(128)}, s32[]{:T(128)}, s32[]{:T(128)}, s32[]{:T(128)}) while((s32[]{:T(128)}, f32[8,128,128]{2,1,0:T(8,128)S(1)}, s32[]{:T(128)}, f32[4,8]{1,0:T(4,128)}, ...), condition=%wide.region_6.7_spmd.clone, body=%wide.region_5.6_spmd.clone.sunk | while | flops 524296 | bytes 1573127 | solution.py:22
  62.9 0.7 dynamic-slice_bitcast_fusion.5
  63.6 1.2 fusion.114
  64.8 0.7 dynamic-slice_bitcast_fusion.5
  65.5 1.2 fusion.114
  66.7 0.7 dynamic-slice_bitcast_fusion.5
  67.4 1.2 fusion.114
  68.6 0.7 dynamic-slice_bitcast_fusion.5
  69.3 1.2 fusion.114
  70.5 0.6 fusion.10
  71.3 0.4 fusion.44
  71.9 9.8 %all-reduce.2 = (f32[16,4]{0,1:T(4,128)S(1)}, f32[16,4]{0,1:T(4,128)S(1)}) all-reduce(f32[16,4]{0,1:T(4,128)S(1)} %fusion.55, f32[16,4]{0,1:T(4,128)S(1)} %fusion.66), channel_id=1, replica_groups=mesh['seq'=4,'head'=4,'dp'=2] {'head'}, use_global_device_ids=true, to_apply=%region_2.0 | all-reduce | flops 128 | bytes 1024 | tf_op jit(solution)/shard_map/psum | solution.py:76
  82.1 0.4 fusion.19
  82.5 1.2 fusion.23
  84.3 8.6 %psum.60 = f32[4,2]{1,0:T(4,128)} all-reduce(f32[4,2]{1,0:T(4,128)S(1)} %fusion.68), channel_id=1, replica_groups=mesh['seq'=4,'head'=4,'dp'=2] {'head'}, use_global_device_ids=true, to_apply=%region_8.9 | all-reduce | flops 8 | bytes 64 | tf_op jit(solution)/shard_map/psum | solution.py:135
  92.9 0.6 reduce_sum.9
  93.8 1.1 fusion.16
  94.9 0.7 fusion.9
  95.8 0.9 copy.62
  97.0 28.4 %all-reduce.1 = (f32[4,1024]{1,0:T(4,128)}, f32[4,1024]{1,0:T(4,128)}, f32[4]{0:T(128)}) all-reduce(f32[4,1024]{1,0:T(4,128)S(1)} %convolution_subtract_fusion, f32[4,1024]{1,0:T(4,128)S(1)} %fusion.67, f32[4]{0:T(128)S(1)} %copy-done.18), channel_id=1, replica_groups=mesh['seq'=4,'head'=4,'dp'=2] {'seq','dp'}, use_global_device_ids=true, to_apply=%region_9.10 | all-reduce | flops 8196 | bytes 65568 | tf_op jit(solution)/shard_map/psum | solution.py:141
  125.7 1.1 fusion.18
  126.8 1.3 all-gather.6.cloned.1.call-done
  128.1 7.5 %while.30 = (s32[]{:T(128)}, f32[8,128,128]{2,1,0:T(8,128)S(1)}, s32[]{:T(128)}, f32[4,8]{1,0:T(4,128)}, f32[4,8,128,128]{3,2,1,0:T(8,128)}, /*index=5*/s32[]{:T(128)}, s32[]{:T(128)}) while((s32[]{:T(128)}, f32[8,128,128]{2,1,0:T(8,128)S(1)}, s32[]{:T(128)}, f32[4,8]{1,0:T(4,128)}, f32[4,8,128,128]{3,2,1,0:T(8,128)}, ...), condition=%wide.region_4.5_spmd.clone, body=%wide.region_3.4_spmd.clone.sunk | while | flops 524292 | bytes 1573065 | solution.py:22
  128.1 0.7 dynamic-slice_bitcast_fusion.4
  128.7 1.2 fusion.113
  129.9 0.7 dynamic-slice_bitcast_fusion.4
  130.6 1.2 fusion.113
  131.8 0.7 dynamic-slice_bitcast_fusion.4
  132.5 1.2 fusion.113
  133.7 0.7 dynamic-slice_bitcast_fusion.4
  134.4 1.2 fusion.113
  135.6 0.4 fusion.8
  135.9 0.6 fusion.7
  136.9 0.9 copy.61
  137.7 0.3 fusion.17
  138.0 0.9 copy.60
  (75 shorter events, 4.2 us)
Async XLA Ops:
  7.2 6.8 %copy-start = (f32[1024,2]{0,1:T(2,128)S(1)}, f32[1024,2]{0,1:T(2,128)}, u32[]{:S(2)}) copy-start(f32[1024,2]{0,1:T(2,128)} %param.20) | copy-start | bytes 24580
  7.2 6.8 %copy-start.8 = (f32[4,1024]{1,0:T(4,128)S(1)}, f32[4,1024]{1,0:T(4,128)}, u32[]{:S(2)}) copy-start(f32[4,1024]{1,0:T(4,128)} %param.19) | copy-start | bytes 49156
  7.2 34.5 %copy-start.4 = (bf16[1,128,1024]{2,1,0:T(8,128)(2,1)S(1)}, bf16[1,128,1024]{2,1,0:T(8,128)(2,1)}, u32[]{:S(2)}) copy-start(bf16[1,128,1024]{2,1,0:T(8,128)(2,1)} %param.15) | copy-start | bytes 786436
  7.2 37.9 %copy-start.13 = (s32[1,16]{1,0:T(1,128)S(1)}, s32[1,16]{1,0:T(1,128)}, u32[]{:S(2)}) copy-start(s32[1,16]{1,0:T(1,128)} %param.23) | copy-start | bytes 196
  7.2 37.9 %copy-start.1 = (bf16[1,128,1024]{2,1,0:T(8,128)(2,1)S(1)}, bf16[1,128,1024]{2,1,0:T(8,128)(2,1)}, u32[]{:S(2)}) copy-start(bf16[1,128,1024]{2,1,0:T(8,128)(2,1)} %param.16) | copy-start | bytes 786436
  7.2 55.7 %all-gather.8.cloned.1.call-start = ((), (), s32[]{:S(2)}) async-start(), calls=%async_computation.1 | async-start | bytes 2621440 | tf_op jit(solution)/shard_map/all_gather | solution.py:11
  7.3 38.1 %copy-start.5 = (f32[4,1024]{1,0:T(4,128)S(1)}, f32[4,1024]{1,0:T(4,128)}, u32[]{:S(2)}) copy-start(f32[4,1024]{1,0:T(4,128)} %param.21) | copy-start | bytes 49156
  12.3 50.6 %copy-start.19 = (f32[8]{0:T(128)}, f32[8]{0:T(128)S(1)}, u32[]{:S(2)}) copy-start(f32[8]{0:T(128)S(1)} %get-tuple-element.320) | copy-start | bytes 100
  13.9 114.2 %all-gather.6.cloned.1.call-start = ((), (), s32[]{:S(2)}) async-start(), calls=%async_computation | async-start | bytes 2621440 | tf_op jit(solution)/shard_map/all_gather | solution.py:11
  43.3 38.7 %copy-start.15 = (s32[128]{0:T(128)}, s32[128]{0:T(128)S(1)}, u32[]{:S(2)}) copy-start(s32[128]{0:T(128)S(1)} %iota_add_fusion) | copy-start | bytes 1540
  44.7 18.2 %copy-start.10 = (f32[2,2]{1,0:T(2,128)}, f32[2,2]{1,0:T(2,128)S(1)}, u32[]{:S(2)}) copy-start(f32[2,2]{1,0:T(2,128)S(1)} %maximum_divide_fusion) | copy-start | bytes 52
  44.7 26.6 %copy-start.9 = (pred[128,128]{1,0:T(8,128)(4,1)}, pred[128,128]{1,0:T(8,128)(4,1)S(1)}, u32[]{:S(2)}) copy-start(pred[128,128]{1,0:T(8,128)(4,1)S(1)} %fusion.43) | copy-start | bytes 49156
  45.9 25.1 %copy-start.2 = (bf16[8,128,128]{2,1,0:T(8,128)(2,1)}, bf16[8,128,128]{2,1,0:T(8,128)(2,1)S(1)}, u32[]{:S(2)}) copy-start(bf16[8,128,128]{2,1,0:T(8,128)(2,1)S(1)} %fusion.13) | copy-start | bytes 786436
  70.4 11.3 %copy-start.17 = (f32[4]{0:T(128)S(1)}, f32[4]{0:T(128)}, u32[]{:S(2)}) copy-start(f32[4]{0:T(128)} %param.22) | copy-start | bytes 52
  81.7 11.2 %copy-start.6 = (f32[16,4]{0,1:T(4,128)}, f32[16,4]{0,1:T(4,128)S(1)}, u32[]{:S(2)}) copy-start(f32[16,4]{0,1:T(4,128)S(1)} %get-tuple-element.309) | copy-start | bytes 772
  94.8 1.8 %copy-start.11 = (f32[2,2]{1,0:T(2,128)S(1)}, f32[2,2]{1,0:T(2,128)}, u32[]{:S(2)}) copy-start(f32[2,2]{1,0:T(2,128)} %copy-done.10) | copy-start | bytes 52
  94.8 1.8 %copy-start.12 = (f32[4,2]{1,0:T(4,128)S(1)}, f32[4,2]{1,0:T(4,128)}, u32[]{:S(2)}) copy-start(f32[4,2]{1,0:T(4,128)} %psum.60) | copy-start | bytes 100
  94.9 2.1 %copy-start.18 = (f32[4]{0:T(128)S(1)}, f32[4]{0:T(128)}, u32[]{:S(2)}) copy-start(f32[4]{0:T(128)} %reduce_sum.9) | copy-start | bytes 52
  94.9 30.5 %copy-start.7 = (f32[16,4]{0,1:T(4,128)S(1)}, f32[16,4]{0,1:T(4,128)}, u32[]{:S(2)}) copy-start(f32[16,4]{0,1:T(4,128)} %copy-done.6) | copy-start | bytes 772
  94.9 30.8 %copy-start.14 = (s32[1,16]{1,0:T(1,128)S(1)}, s32[1,16]{1,0:T(1,128)}, u32[]{:S(2)}) copy-start(s32[1,16]{1,0:T(1,128)} %param.23) | copy-start | bytes 196
  94.9 30.8 %copy-start.16 = (s32[128]{0:T(128)S(1)}, s32[128]{0:T(128)}, u32[]{:S(2)}) copy-start(s32[128]{0:T(128)} %copy-done.15) | copy-start | bytes 1540
  135.5 2.2 %copy-start.3 = (bf16[8,128,128]{2,1,0:T(8,128)(2,1)S(1)}, bf16[8,128,128]{2,1,0:T(8,128)(2,1)}, u32[]{:S(2)}) copy-start(bf16[8,128,128]{2,1,0:T(8,128)(2,1)} %copy-done.2) | copy-start | bytes 786436
Sparse Core Ops, SparseCore 0:
  14.0 48.8 all-gather.7
  83.9 44.1 all-gather.5
where the time goes:
time: 147 us; the launch traced here: 146 us
  blocking collectives  70.4 us (48%)
  between operations  19.1 us (13%)
  waiting for transfers between devices  18.3 us (12%)
  local copies, waits for them, and re-layouts  13.5 us (9%)
  other arithmetic  12.2 us (8%)
  matrix products  12 us (8%)
    psum x1, blocking collectives, shards(): lax.psum((weight_part, bias_part, rotation_part), ('seq', 'dp'))  28.4 us
    all_gather x2, waiting for transfers between devices, carried_in(): everything = jax.tree.map(lambda part: lax.all_gather(part, axis), x)  18.3 us
    unnamed x1, blocking collectives  12.2 us
    psum x1, blocking collectives, shards(): gram, coupling = lax.psum((gram_part, coupling_part), 'head')  11.4 us
    psum x1, blocking collectives, shards(): lax.psum(jnp.dot(picked, (proj_weight - rotated).T, precision=highest), '...  9.83 us
    select_n x8, other arithmetic, lap(): return jax.tree.map(lambda a, b: jnp.where(reached, a, b), new, before)  9.35 us
    psum x1, blocking collectives, shards(): lax.psum(jnp.dot(rotated_grad, refusal, precision=highest), 'head')  8.63 us
    mul x8, local copies, waits for them, and re-layouts, chain_combine(): later[0][:, None, None] * earlier[1] + later[1]  5.52 us
  transfers between devices with their start and end apart: 2, of which 2 were waited for; matrix products, arithmetic and copies ran while one was open for 7% of the time, Pallas kernels for 0%

commit v1 on v0

v1 whole, which is shorter than its diff:
```python
import functools
import jax
import jax.numpy as jnp
from jax import lax
from jax.experimental import pallas as pl
from jax.experimental.pallas import tpu as pltpu
from jax.sharding import PartitionSpec as P

highest = lax.Precision.HIGHEST
MESH = pl.DeviceIdType.MESH
f32 = jnp.float32
bf16 = jnp.bfloat16


def contract(a, b, da, db, precision=None):
    return lax.dot_general(
        a, b, (((da,), (db,)), ((), ())), precision=precision, preferred_element_type=f32
    )


def split(x):
    high = x.astype(bf16)
    return high, (x - high.astype(f32)).astype(bf16)


def halves(x):
    n = x.shape[1] // 2
    return x[:, :n] + x[:, n:]


def kernel(
    sizes,
    q_ref,
    k_ref,
    v_ref,
    g_ref,
    decay_ref,
    rotation_ref,
    refusal_ref,
    weight_ref,
    bias_ref,
    positions_ref,
    attended_ref,
    grad_query_ref,
    grad_key_ref,
    grad_value_ref,
    grad_rotation_ref,
    grad_weight_ref,
    grad_bias_ref,
    stack,
    picks,
    rows,
    moved,
    table,
    mixing,
    grad_mixing,
    grad_moved,
    state,
    state_in,
    later,
    later_in,
    first,
    second,
    pay,
    parts,
    total,
    first_send,
    first_recv,
    second_send,
    second_recv,
    state_send,
    state_recv,
    later_send,
    later_recv,
    parts_send,
    parts_recv,
    total_send,
    total_recv,
):
    seqs, peers, docs, heads, owners = sizes
    group = q_ref.shape[1]
    size = q_ref.shape[2] // heads
    npos = positions_ref.shape[1]
    members = seqs * docs
    stride = members // owners
    z, y, c = lax.axis_index("seq"), lax.axis_index("head"), lax.axis_index("dp")
    last = seqs - 1
    member = z * docs + c

    barrier = pltpu.get_barrier_semaphore()
    for step in range(1, peers):
        pl.semaphore_signal(
            barrier, inc=1, device_id={"head": lax.rem(y + step, peers)}, device_id_type=MESH
        )

    def greet(step, carry):
        other = lax.rem(member + step, members)
        pl.semaphore_signal(
            barrier,
            inc=1,
            device_id={"seq": other // docs, "dp": lax.rem(other, docs)},
            device_id_type=MESH,
        )
        return carry

    lax.fori_loop(1, members, greet, 0)

    places = z * group + lax.broadcasted_iota(jnp.int32, (group, npos), 0)
    chosen = places == positions_ref[...]
    select = jnp.where(chosen, 1.0, 0.0)
    stack[npos:, :] = jnp.zeros((stack.shape[0] - npos, stack.shape[1]), f32)
    picked = contract(select.astype(bf16), v_ref[0], 0, 0)
    stack[:npos, :] = picked
    stack[npos : npos + 4, :] = weight_ref[...]
    stack[npos + 4 : npos + 8, :] = rotation_ref[...]
    stack[npos + 8 : npos + 10, :] = refusal_ref[...]
    first[y] = jnp.zeros(first.shape[1:], f32)
    first[y, :, : stack.shape[0]] = contract(stack[npos:, :], stack[...], 1, 1, highest)
    pl.semaphore_wait(barrier, peers - 1 + members - 1)

    def across(buffer, send, recv, step):
        other = lax.rem(y + step, peers)
        return pltpu.make_async_remote_copy(
            src_ref=buffer.at[y],
            dst_ref=buffer.at[y],
            send_sem=send.at[step - 1],
            recv_sem=recv.at[y],
            device_id={"head": other},
            device_id_type=MESH,
        )

    def arrived(buffer, send, recv, step):
        other = lax.rem(y + step, peers)
        pltpu.make_async_remote_copy(
            src_ref=buffer.at[other],
            dst_ref=buffer.at[other],
            send_sem=send.at[step - 1],
            recv_sem=recv.at[other],
            device_id={"head": other},
            device_id_type=MESH,
        ).wait_recv()

    for step in range(1, peers):
        across(first, first_send, first_recv, step).start()

    def state_copy(h):
        return pltpu.make_async_remote_copy(
            src_ref=state.at[h],
            dst_ref=state_in.at[h],
            send_sem=state_send.at[h],
            recv_sem=state_recv.at[h],
            device_id={"seq": lax.rem(z + 1, seqs)},
            device_id_type=MESH,
        )

    def later_copy(h):
        return pltpu.make_async_remote_copy(
            src_ref=later.at[h],
            dst_ref=later_in.at[h],
            send_sem=later_send.at[h],
            recv_sem=later_recv.at[h],
            device_id={"seq": lax.rem(z + seqs - 1, seqs)},
            device_id_type=MESH,
        )

    offsets = lax.broadcasted_iota(jnp.int32, (group, size), 0).astype(f32)

    def log_decay(h):
        return jnp.log1p(-jnp.full((1, size), decay_ref[h], f32))

    for h in range(heads):
        at = slice(h * size, (h + 1) * size)
        weighted = g_ref[0, :, at].astype(f32) * jnp.exp(offsets * log_decay(h))
        both = jnp.concatenate(split(weighted), axis=1)
        later[h] = halves(contract(q_ref[0, :, at], both, 0, 0))

        @pl.when(z == last)
        def _():
            later_copy(h).start()

    @pl.when(z == last)
    def _():
        later_in[...] = jnp.zeros_like(later_in)

    @pl.when(z == 0)
    def _():
        state_in[...] = jnp.zeros_like(state_in)

    columns = lax.broadcasted_iota(jnp.int32, (group, group), 1)
    between = lax.broadcasted_iota(jnp.int32, (group, group), 0) - columns
    apart = jnp.maximum(between, 0).astype(f32)
    for h in range(heads):
        at = slice(h * size, (h + 1) * size)
        powers = jnp.where(between >= 0, jnp.exp(apart * log_decay(h)), 0.0)
        table[h] = powers
        mixing[h] = (contract(q_ref[0, :, at], k_ref[0, :, at], 1, 1) * powers).astype(bf16)

    for step in range(1, peers):
        arrived(first, first_send, first_recv, step)
    summed = first[0]
    for peer in range(1, peers):
        summed = summed + first[peer]
    at_ref = npos + 8
    gram = [
        [summed[8 + a : 9 + a, at_ref + b : at_ref + b + 1] for b in range(2)] for a in range(2)
    ]
    determinant = gram[0][0] * gram[1][1] - gram[0][1] * gram[1][0]
    inverse = [
        [gram[1][1] / determinant, -gram[0][1] / determinant],
        [-gram[1][0] / determinant, gram[0][0] / determinant],
    ]
    coupling = [summed[4:8, at_ref + b : at_ref + b + 1] for b in range(2)]
    map_0 = coupling[0] * inverse[0][0] + coupling[1] * inverse[1][0]
    map_1 = coupling[0] * inverse[0][1] + coupling[1] * inverse[1][1]
    rotated = rotation_ref[...] - map_0 * refusal_ref[0:1, :] - map_1 * refusal_ref[1:2, :]
    rows[...] = jnp.zeros_like(rows)
    rows[0:4, :] = rotated
    rows[4:6, :] = refusal_ref[...]
    along = summed[8:10, :npos]
    rank = lax.broadcasted_iota(jnp.int32, (4, npos), 0)
    bias = jnp.zeros((4, npos), f32)
    for r in range(4):
        bias = jnp.where(rank == r, bias_ref[r], bias)
    code = (
        summed[0:4, :npos]
        + bias
        - (summed[4:8, :npos] - map_0 * along[0:1, :] - map_1 * along[1:2, :])
    )
    spread = contract(select, code, 1, 1, highest)
    for h in range(heads):
        at = slice(h * size, (h + 1) * size)
        value = v_ref[0, :, at].astype(f32)
        shift = spread[:, 0:1] * rows[0:1, at]
        for r in range(1, 4):
            shift = shift + spread[:, r : r + 1] * rows[r : r + 1, at]
        value = (value + shift).astype(bf16)
        moved[:, at] = value
        weighted = value.astype(f32) * jnp.exp((group - 1.0 - offsets) * log_decay(h))
        both = jnp.concatenate(split(weighted), axis=1)
        state[h] = halves(contract(k_ref[0, :, at], both, 0, 0))

        @pl.when(z == 0)
        def _():
            state_copy(h).start()

    def later_step(h):
        at = pl.ds(pl.multiple_of(h * size, size), size)
        decay = log_decay(h)

        @pl.when(z < last)
        def _():
            later_copy(h).wait_recv()

        @pl.when(jnp.logical_and(z > 0, z < last))
        def _():
            later[h] = later[h] + jnp.exp(group * decay) * later_in[h]
            later_copy(h).start()

        high, low = split(later_in[h])
        leave = jnp.exp((group - offsets) * decay)
        grad = g_ref[0, :, at]
        value = moved[:, at]
        wide = contract(mixing[h], grad, 0, 0) + leave * halves(
            contract(k_ref[0, :, at], jnp.concatenate([high, low], axis=1), 1, 0)
        )
        grad_moved[:, at] = wide
        picks[:npos, at] = contract(select, wide, 0, 0, highest)
        mixed = (contract(grad, value, 1, 1) * table[h]).astype(bf16)
        grad_mixing[h] = mixed
        grad_key = contract(mixed, q_ref[0, :, at], 0, 0) + leave * halves(
            contract(value, jnp.concatenate([high, low], axis=0), 1, 1)
        )
        grad_key_ref[0, :, at] = grad_key.astype(bf16)

    def state_step(h):
        at = pl.ds(pl.multiple_of(h * size, size), size)
        decay = log_decay(h)

        @pl.when(z > 0)
        def _():
            state_copy(h).wait_recv()

        @pl.when(jnp.logical_and(z > 0, z < last))
        def _():
            state[h] = state[h] + jnp.exp(group * decay) * state_in[h]
            state_copy(h).start()

        high, low = split(state_in[h])
        enter = jnp.exp((offsets + 1.0) * decay)
        attended = contract(mixing[h], moved[:, at], 1, 0) + enter * halves(
            contract(q_ref[0, :, at], jnp.concatenate([high, low], axis=1), 1, 0)
        )
        attended_ref[0, :, at] = attended.astype(bf16)
        grad_query = contract(grad_mixing[h], k_ref[0, :, at], 1, 0) + enter * halves(
            contract(g_ref[0, :, at], jnp.concatenate([high, low], axis=0), 1, 1)
        )
        grad_query_ref[0, :, at] = grad_query.astype(bf16)

    lag = jnp.clip(2 * (2 * z - last) + 3, 0, heads)

    def both_steps(i, carry):
        later_step(i)

        @pl.when(i >= lag)
        def _():
            state_step(jnp.maximum(i - lag, 0))

        return carry

    lax.fori_loop(0, heads, both_steps, 0)

    second[y] = jnp.zeros(second.shape[1:], f32)
    second[y, :, :npos] = contract(rows[...], picks[:npos, :], 1, 1, highest)
    for step in range(1, peers):
        across(second, second_send, second_recv, step).start()

    def part_copy(owner):
        target = owner * stride
        return pltpu.make_async_remote_copy(
            src_ref=pay.at[owner],
            dst_ref=parts.at[member],
            send_sem=parts_send.at[owner],
            recv_sem=parts_recv.at[member],
            device_id={"seq": target // docs, "dp": target % docs},
            device_id_type=MESH,
        )

    def finish_code():
        for step in range(1, peers):
            arrived(second, second_send, second_recv, step)
        sums = second[0]
        for peer in range(1, peers):
            sums = sums + second[peer]
        code_grad = sums[0:4, :npos]
        ahead = sums[4:6, :npos]
        projected = [
            jnp.sum(
                code * ahead[b : b + 1, :] - code_grad * along_own[b : b + 1, :],
                axis=1,
                keepdims=True,
            )
            for b in range(2)
        ]
        back_0 = projected[0] * inverse[0][0] + projected[1] * inverse[1][0]
        back_1 = projected[0] * inverse[0][1] + projected[1] * inverse[1][1]
        weight_part = contract(code_grad, stack[:npos, :], 1, 0, highest)
        rotation_part = (
            contract(code, picks[:npos, :], 1, 0, highest)
            - weight_part
            - back_0 * refusal_ref[0:1, :]
            - back_1 * refusal_ref[1:2, :]
        )
        bias_part = jnp.sum(code_grad, axis=1, keepdims=True)
        width = pay.shape[2]
        for owner in range(owners):
            at = slice(owner * width, (owner + 1) * width)
            pay[owner, 0:4, :] = rotation_part[:, at]
            pay[owner, 4:8, :] = weight_part[:, at]
            pay[owner, 8:12, :] = jnp.broadcast_to(bias_part, (4, width))
            pay[owner, 12:16, :] = jnp.zeros((4, width), f32)

            @pl.when(member == owner * stride)
            def _():
                parts[member] = pay[owner]

            @pl.when(member != owner * stride)
            def _():
                part_copy(owner).start()

        spread_grad = contract(select, code_grad, 1, 1, highest)
        for h in range(heads):
            at = slice(h * size, (h + 1) * size)
            wide = grad_moved[:, at]
            for r in range(4):
                wide = wide + spread_grad[:, r : r + 1] * (
                    weight_ref[r : r + 1, at] - rows[r : r + 1, at]
                )
            grad_value_ref[0, :, at] = wide.astype(bf16)

    along_own = along

    @pl.when(z == last)
    def _():
        finish_code()

    def rest(i, carry):
        state_step(i - lag)
        return carry

    lax.fori_loop(heads, heads + lag, rest, 0)

    @pl.when(z < last)
    def _():
        finish_code()

    mine = member // stride
    owning = lax.rem(member, stride) == 0

    def total_copy(step):
        other = lax.rem(member + step, members)
        return pltpu.make_async_remote_copy(
            src_ref=total.at[mine],
            dst_ref=total.at[mine],
            send_sem=total_send.at[step],
            recv_sem=total_recv.at[mine],
            device_id={"seq": other // docs, "dp": lax.rem(other, docs)},
            device_id_type=MESH,
        )

    def part_arrived(step, carry):
        other = lax.rem(member + step, members)
        pltpu.make_async_remote_copy(
            src_ref=pay.at[0],
            dst_ref=parts.at[other],
            send_sem=parts_send.at[0],
            recv_sem=parts_recv.at[other],
            device_id={"seq": other // docs, "dp": lax.rem(other, docs)},
            device_id_type=MESH,
        ).wait_recv()
        return carry

    def total_start(step, carry):
        total_copy(step).start()
        return carry

    def total_sent(step, carry):
        total_copy(step).wait_send()
        return carry

    @pl.when(owning)
    def _():
        lax.fori_loop(1, members, part_arrived, 0)
        total[mine] = jnp.sum(parts[...], axis=0)
        lax.fori_loop(1, members, total_start, 0)

    width = pay.shape[2]
    for owner in range(owners):

        @pl.when(member != owner * stride)
        def _():
            pltpu.make_async_remote_copy(
                src_ref=total.at[owner],
                dst_ref=total.at[owner],
                send_sem=total_send.at[0],
                recv_sem=total_recv.at[owner],
                device_id={"seq": (owner * stride) // docs, "dp": (owner * stride) % docs},
                device_id_type=MESH,
            ).wait_recv()

    for owner in range(owners):
        at = slice(owner * width, (owner + 1) * width)
        grad_rotation_ref[:, at] = total[owner, 0:4, :]
        grad_weight_ref[:, at] = total[owner, 4:8, :]
    for r in range(4):
        grad_bias_ref[r] = jnp.sum(total[0, 8 + r : 9 + r, 0:1])

    for step in range(1, peers):
        across(first, first_send, first_recv, step).wait_send()
        across(second, second_send, second_recv, step).wait_send()

    def sent(h, carry):
        @pl.when(z < last)
        def _():
            state_copy(h).wait_send()

        @pl.when(z > 0)
        def _():
            later_copy(h).wait_send()

        return carry

    lax.fori_loop(0, heads, sent, 0)
    for owner in range(owners):

        @pl.when(member != owner * stride)
        def _():
            part_copy(owner).wait_send()

    @pl.when(owning)
    def _():
        lax.fori_loop(1, members, total_sent, 0)


def shards(mesh, *arrays):
    (queries, key_rows, values, out_grad, decay_rate, rotation, refusal, weight, bias, positions) = (
        arrays
    )
    seqs, peers, docs = mesh.shape["seq"], mesh.shape["head"], mesh.shape["dp"]
    heads = decay_rate.shape[0]
    group, width = queries.shape[1], queries.shape[2]
    size = width // heads
    npos = positions.shape[1]
    members = seqs * docs
    owners = min(members, width // 128)
    vmem = pl.BlockSpec(memory_space=pltpu.VMEM)
    smem = pl.BlockSpec(memory_space=pltpu.SMEM)
    dma = pltpu.SemaphoreType.DMA
    square = (heads, size, size)
    big = jax.ShapeDtypeStruct(queries.shape, bf16)
    return pl.pallas_call(
        functools.partial(kernel, (seqs, peers, docs, heads, owners)),
        out_shape=(
            big,
            big,
            big,
            big,
            jax.ShapeDtypeStruct(rotation.shape, f32),
            jax.ShapeDtypeStruct(weight.shape, f32),
            jax.ShapeDtypeStruct(bias.shape, f32),
        ),
        in_specs=[vmem, vmem, vmem, vmem, smem, vmem, vmem, vmem, smem, vmem],
        out_specs=(vmem, vmem, vmem, vmem, vmem, vmem, smem),
        scratch_shapes=[
            pltpu.VMEM((npos + 16, width), f32),
            pltpu.VMEM((npos, width), f32),
            pltpu.VMEM((8, width), f32),
            pltpu.VMEM((group, width), bf16),
            pltpu.VMEM((heads, group, group), f32),
            pltpu.VMEM((heads, group, group), bf16),
            pltpu.VMEM((heads, group, group), bf16),
            pltpu.VMEM((group, width), f32),
            pltpu.VMEM(square, f32),
            pltpu.VMEM(square, f32),
            pltpu.VMEM(square, f32),
            pltpu.VMEM(square, f32),
            pltpu.VMEM((peers, 16, 128), f32),
            pltpu.VMEM((peers, 8, 128), f32),
            pltpu.VMEM((owners, 16, width // owners), f32),
            pltpu.VMEM((members, 16, width // owners), f32),
            pltpu.VMEM((owners, 16, width // owners), f32),
            dma((peers,)),
            dma((peers,)),
            dma((peers,)),
            dma((peers,)),
            dma((heads,)),
            dma((heads,)),
            dma((heads,)),
            dma((heads,)),
            dma((owners,)),
            dma((members,)),
            dma((members,)),
            dma((owners,)),
        ],
        compiler_params=pltpu.CompilerParams(
            collective_id=0, has_side_effects=True, vmem_limit_bytes=40 * 1024 * 1024
        ),
    )(queries, key_rows, values, out_grad, decay_rate, rotation, refusal.T, weight, bias, positions)


def solution(mesh):
    return jax.shard_map(
        functools.partial(shards, mesh),
        mesh=mesh,
        in_specs=(
            P("dp", "seq", "head"),
            P("dp", "seq", "head"),
            P("dp", "seq", "head"),
            P("dp", "seq", "head"),
            P("head"),
            P(None, "head"),
            P("head", None),
            P(None, "head"),
            P(),
            P("dp", None),
        ),
        out_specs=(
            P("dp", "seq", "head"),
            P("dp", "seq", "head"),
            P("dp", "seq", "head"),
            P("dp", "seq", "head"),
            P(None, "head"),
            P(None, "head"),
            P(),
        ),
        check_vma=False,
    )
```

time: 147 us -> 53.9 us (0.37)
  blocking collectives: 70.4 us -> 0 us
  Pallas kernels: 0 us -> 41.7 us
  between operations: 19.1 us -> 0.68 us
  waiting for transfers between devices: 18.3 us -> 0 us
  other arithmetic: 12.2 us -> 0 us
  matrix products: 12 us -> 0 us
  local copies, waits for them, and re-layouts: 13.5 us -> 11.1 us
    psum x4 -> x0, blocking collectives: 58.2 us -> none  [the longest x1 28.4 us: shards(): lax.psum((weight_part, bias_part, rotation_part), ('seq', 'dp'))]
    pallas_call x0 -> x1, Pallas kernels: none -> 41.7 us  [shards(): pl.pallas_call(functools.partial(kernel, (seqs, peers, docs, heads, owner...]
    all_gather x2 -> x0, waiting for transfers between devices: 18.3 us -> none  [carried_in(): everything = jax.tree.map(lambda part: lax.all_gather(part, axis), x)]
    unnamed x1 -> x0, blocking collectives: 12.2 us -> none
    dot_general x29 -> x0, matrix products: 12 us -> none  [the longest x1 1.48 us: shards(): jnp.einsum('thd,the->hde', query_full * start_weight[:, :, None], grad_fu...]
    select_n x8 -> x0, other arithmetic: 9.35 us -> none  [lap(): return jax.tree.map(lambda a, b: jnp.where(reached, a, b), new, before)]
    unnamed x46 -> x27, local copies, waits for them, and re-layouts: 3.97 us -> 11.1 us
    mul x8 -> x0, local copies, waits for them, and re-layouts: 5.52 us -> none  [chain_combine(): later[0][:, None, None] * earlier[1] + later[1]]
  transfers between devices with their start and end apart: 2 -> 0, of which waited for: 2 -> 0; matrix products, arithmetic and copies ran while one was open for 7% -> 0% of each run, Pallas kernels for 0% -> 0%
where the time goes in v1:
time: 53.9 us; the launch traced here: 53.5 us
  Pallas kernels  41.7 us (77%)
  local copies, waits for them, and re-layouts  11.1 us (21%)
  between operations  0.68 us (1%)
    pallas_call x1, Pallas kernels, shards(): pl.pallas_call(functools.partial(kernel, (seqs, peers, docs, heads, owner...  41.7 us
    unnamed x27, local copies, waits for them, and re-layouts  11.1 us

profile of v1, /device:TPU:0, one launch (start us, length us, event | category | flops | bytes accessed | tf_op | source)
XLA Modules:
  0.0 53.5 jit_solution(14913020368269252349)
XLA Ops:
  0.6 0.0 copy-start.9
  0.6 0.0 copy-start.8
  0.7 0.0 copy-start.7
  0.7 0.6 %copy-done.9 = s32[1,16]{1,0:T(1,128)S(1)} copy-done((s32[1,16]{1,0:T(1,128)S(1)}, s32[1,16]{1,0:T(1,128)}, u32[]{:S(2)}) %copy-start.9) | copy-done | bytes 88
  1.3 0.0 copy-done.8
  1.3 0.0 copy-done.7
  1.3 0.0 copy-start
  1.3 0.9 %copy-done = bf16[1,128,1024]{2,1,0:T(8,128)(2,1)S(1)} copy-done((bf16[1,128,1024]{2,1,0:T(8,128)(2,1)S(1)}, bf16[1,128,1024]{2,1,0:T(8,128)(2,1)}, u32[]{:S(2)}) %copy-start) | copy-done | bytes 262168
  2.3 0.0 copy-start.1
  2.3 0.9 %copy-done.1 = bf16[1,128,1024]{2,1,0:T(8,128)(2,1)S(1)} copy-done((bf16[1,128,1024]{2,1,0:T(8,128)(2,1)S(1)}, bf16[1,128,1024]{2,1,0:T(8,128)(2,1)}, u32[]{:S(2)}) %copy-start.1) | copy-done | bytes 262168
  3.2 0.0 copy-start.2
  3.2 0.9 %copy-done.2 = bf16[1,128,1024]{2,1,0:T(8,128)(2,1)S(1)} copy-done((bf16[1,128,1024]{2,1,0:T(8,128)(2,1)S(1)}, bf16[1,128,1024]{2,1,0:T(8,128)(2,1)}, u32[]{:S(2)}) %copy-start.2) | copy-done | bytes 262168
  4.2 0.0 copy-start.3
  4.2 0.9 %copy-done.3 = bf16[1,128,1024]{2,1,0:T(8,128)(2,1)S(1)} copy-done((bf16[1,128,1024]{2,1,0:T(8,128)(2,1)S(1)}, bf16[1,128,1024]{2,1,0:T(8,128)(2,1)}, u32[]{:S(2)}) %copy-start.3) | copy-done | bytes 262168
  5.1 0.0 copy-start.4
  5.1 0.7 %copy-done.4 = f32[4,1024]{1,0:T(4,128)S(1)} copy-done((f32[4,1024]{1,0:T(4,128)S(1)}, f32[4,1024]{1,0:T(4,128)}, u32[]{:S(2)}) %copy-start.4) | copy-done | bytes 16408
  5.8 0.0 copy-start.5
  5.8 0.7 %copy-done.5 = f32[4,1024]{1,0:T(4,128)S(1)} copy-done((f32[4,1024]{1,0:T(4,128)S(1)}, f32[4,1024]{1,0:T(4,128)}, u32[]{:S(2)}) %copy-start.5) | copy-done | bytes 16408
  6.6 0.0 copy-start.6
  6.6 0.7 %copy-done.6 = f32[1024,2]{0,1:T(2,128)S(1)} copy-done((f32[1024,2]{0,1:T(2,128)S(1)}, f32[1024,2]{0,1:T(2,128)}, u32[]{:S(2)}) %copy-start.6) | copy-done | bytes 8216
  7.3 41.7 %shard_map.153 = (bf16[1,128,1024]{2,1,0:T(8,128)(2,1)S(1)}, bf16[1,128,1024]{2,1,0:T(8,128)(2,1)S(1)}, bf16[1,128,1024]{2,1,0:T(8,128)(2,1)S(1)}, bf16[1,128,10...) custom-call(bf16[1,128,1024]{2,1,0:T(8,128)(2,1)S(1)} %copy-done, ...), custom_call_target="tpu_custom_call" | custom-call | tf_op jit(solution)/shard_map/pallas_call | solution.py:500
  49.0 0.7 %copy.24 = bf16[1,128,1024]{2,1,0:T(8,128)(2,1)} copy(bf16[1,128,1024]{2,1,0:T(8,128)(2,1)S(1)} %get-tuple-element.14) | data formatting | bytes 524288
  49.7 0.7 %copy.25 = bf16[1,128,1024]{2,1,0:T(8,128)(2,1)} copy(bf16[1,128,1024]{2,1,0:T(8,128)(2,1)S(1)} %get-tuple-element.15) | data formatting | bytes 524288
  50.4 0.7 %copy.26 = bf16[1,128,1024]{2,1,0:T(8,128)(2,1)} copy(bf16[1,128,1024]{2,1,0:T(8,128)(2,1)S(1)} %get-tuple-element.16) | data formatting | bytes 524288
  51.1 0.7 %copy.27 = bf16[1,128,1024]{2,1,0:T(8,128)(2,1)} copy(bf16[1,128,1024]{2,1,0:T(8,128)(2,1)S(1)} %get-tuple-element.17) | data formatting | bytes 524288
  51.8 0.6 %copy.28 = f32[4,1024]{1,0:T(4,128)} copy(f32[4,1024]{1,0:T(4,128)S(1)} %get-tuple-element.18) | data formatting | bytes 32768
  52.4 0.6 %copy.29 = f32[4,1024]{1,0:T(4,128)} copy(f32[4,1024]{1,0:T(4,128)S(1)} %get-tuple-element.19) | data formatting | bytes 32768
  53.0 0.5 copy.30
Async XLA Ops:
  0.6 0.7 %copy-start.9 = (s32[1,16]{1,0:T(1,128)S(1)}, s32[1,16]{1,0:T(1,128)}, u32[]{:S(2)}) copy-start(s32[1,16]{1,0:T(1,128)} %positions_ref.1) | copy-start | bytes 196
  0.6 0.7 %copy-start.8 = (f32[4]{0:T(128)S(1)}, f32[4]{0:T(128)}, u32[]{:S(2)}) copy-start(f32[4]{0:T(128)} %bias_ref.1) | copy-start | bytes 52
  0.7 0.7 %copy-start.7 = (f32[8]{0:T(128)S(1)}, f32[8]{0:T(128)}, u32[]{:S(2)}) copy-start(f32[8]{0:T(128)} %decay_ref.1) | copy-start | bytes 100
  1.3 0.9 %copy-start = (bf16[1,128,1024]{2,1,0:T(8,128)(2,1)S(1)}, bf16[1,128,1024]{2,1,0:T(8,128)(2,1)}, u32[]{:S(2)}) copy-start(bf16[1,128,1024]{2,1,0:T(8,128)(2,1)} %q_ref.1) | copy-start | bytes 786436
  2.3 0.9 %copy-start.1 = (bf16[1,128,1024]{2,1,0:T(8,128)(2,1)S(1)}, bf16[1,128,1024]{2,1,0:T(8,128)(2,1)}, u32[]{:S(2)}) copy-start(bf16[1,128,1024]{2,1,0:T(8,128)(2,1)} %k_ref.1) | copy-start | bytes 786436
  3.2 0.9 %copy-start.2 = (bf16[1,128,1024]{2,1,0:T(8,128)(2,1)S(1)}, bf16[1,128,1024]{2,1,0:T(8,128)(2,1)}, u32[]{:S(2)}) copy-start(bf16[1,128,1024]{2,1,0:T(8,128)(2,1)} %v_ref.1) | copy-start | bytes 786436
  4.2 0.9 %copy-start.3 = (bf16[1,128,1024]{2,1,0:T(8,128)(2,1)S(1)}, bf16[1,128,1024]{2,1,0:T(8,128)(2,1)}, u32[]{:S(2)}) copy-start(bf16[1,128,1024]{2,1,0:T(8,128)(2,1)} %g_ref.1) | copy-start | bytes 786436
  5.1 0.7 %copy-start.4 = (f32[4,1024]{1,0:T(4,128)S(1)}, f32[4,1024]{1,0:T(4,128)}, u32[]{:S(2)}) copy-start(f32[4,1024]{1,0:T(4,128)} %rotation_ref.1) | copy-start | bytes 49156
  5.8 0.7 %copy-start.5 = (f32[4,1024]{1,0:T(4,128)S(1)}, f32[4,1024]{1,0:T(4,128)}, u32[]{:S(2)}) copy-start(f32[4,1024]{1,0:T(4,128)} %weight_ref.1) | copy-start | bytes 49156
  6.6 0.7 %copy-start.6 = (f32[1024,2]{0,1:T(2,128)S(1)}, f32[1024,2]{0,1:T(2,128)}, u32[]{:S(2)}) copy-start(f32[1024,2]{0,1:T(2,128)} %param.16) | copy-start | bytes 24580

commit v2 on v1

--- a/solution.py
+++ b/solution.py
@@ -30,6 +30,31 @@
 
 def kernel(
     sizes,
+    q_in,
+    k_in,
+    v_in,
+    g_in,
+    decay_in,
+    rotation_in,
+    refusal_in,
+    weight_in,
+    bias_in,
+    positions_in,
+    attended_out,
+    grad_query_out,
+    grad_key_out,
+    grad_value_out,
+    grad_rotation_out,
+    grad_weight_out,
+    grad_bias_out,
+    attended_ref,
+    grad_query_ref,
+    grad_key_ref,
+    grad_value_ref,
+    grad_rotation_ref,
+    grad_weight_ref,
+    grad_bias_ref,
+    store_sem,
     q_ref,
     k_ref,
     v_ref,
@@ -40,20 +65,14 @@
     weight_ref,
     bias_ref,
     positions_ref,
-    attended_ref,
-    grad_query_ref,
-    grad_key_ref,
-    grad_value_ref,
-    grad_rotation_ref,
-    grad_weight_ref,
-    grad_bias_ref,
+    load_sem,
+    select_rows,
+    inner,
+    inner_query,
     stack,
     picks,
     rows,
     moved,
-    table,
-    mixing,
-    grad_mixing,
     grad_moved,
     state,
     state_in,
@@ -87,6 +106,39 @@
     last = seqs - 1
     member = z * docs + c
 
+    loads = [
+        pltpu.make_async_copy(source, target, load_sem.at[i])
+        for i, (source, target) in enumerate(
+            (
+                (v_in, v_ref),
+                (positions_in, positions_ref),
+                (weight_in, weight_ref),
+                (rotation_in, rotation_ref),
+                (refusal_in, refusal_ref),
+                (decay_in, decay_ref),
+                (bias_in, bias_ref),
+                (q_in, q_ref),
+                (g_in, g_ref),
+                (k_in, k_ref),
+            )
+        )
+    ]
+    for load in loads:
+        load.start()
+    stores = [
+        pltpu.make_async_copy(source, target, store_sem.at[i])
+        for i, (source, target) in enumerate(
+            (
+                (attended_ref, attended_out),
+                (grad_query_ref, grad_query_out),
+                (grad_key_ref, grad_key_out),
+                (grad_value_ref, grad_value_out),
+                (grad_rotation_ref, grad_rotation_out),
+                (grad_weight_ref, grad_weight_out),
+                (grad_bias_ref, grad_bias_out),
+            )
+        )
+    ]
     barrier = pltpu.get_barrier_semaphore()
     for step in range(1, peers):
         pl.semaphore_signal(
@@ -105,11 +157,15 @@
 
     lax.fori_loop(1, members, greet, 0)
 
+    for load in loads[:5]:
+        load.wait()
     places = z * group + lax.broadcasted_iota(jnp.int32, (group, npos), 0)
     chosen = places == positions_ref[...]
     select = jnp.where(chosen, 1.0, 0.0)
+    turned = select.T
+    select_rows[...] = turned.astype(bf16)
     stack[npos:, :] = jnp.zeros((stack.shape[0] - npos, stack.shape[1]), f32)
-    picked = contract(select.astype(bf16), v_ref[0], 0, 0)
+    picked = contract(select_rows[...], v_ref[0], 1, 0)
     stack[:npos, :] = picked
     stack[npos : npos + 4, :] = weight_ref[...]
     stack[npos + 4 : npos + 8, :] = rotation_ref[...]
@@ -168,6 +224,8 @@
     def log_decay(h):
         return jnp.log1p(-jnp.full((1, size), decay_ref[h], f32))
 
+    for load in loads[5:9]:
+        load.wait()
     for h in range(heads):
         at = slice(h * size, (h + 1) * size)
         weighted = g_ref[0, :, at].astype(f32) * jnp.exp(offsets * log_decay(h))
@@ -186,14 +244,10 @@
     def _():
         state_in[...] = jnp.zeros_like(state_in)
 
-    columns = lax.broadcasted_iota(jnp.int32, (group, group), 1)
-    between = lax.broadcasted_iota(jnp.int32, (group, group), 0) - columns
+    between = lax.broadcasted_iota(jnp.int32, (group, group), 0) - lax.broadcasted_iota(
+        jnp.int32, (group, group), 1
+    )
     apart = jnp.maximum(between, 0).astype(f32)
-    for h in range(heads):
-        at = slice(h * size, (h + 1) * size)
-        powers = jnp.where(between >= 0, jnp.exp(apart * log_decay(h)), 0.0)
-        table[h] = powers
-        mixing[h] = (contract(q_ref[0, :, at], k_ref[0, :, at], 1, 1) * powers).astype(bf16)
 
     for step in range(1, peers):
         arrived(first, first_send, first_recv, step)
@@ -227,6 +281,7 @@
         - (summed[4:8, :npos] - map_0 * along[0:1, :] - map_1 * along[1:2, :])
     )
     spread = contract(select, code, 1, 1, highest)
+    loads[9].wait()
     for h in range(heads):
         at = slice(h * size, (h + 1) * size)
         value = v_ref[0, :, at].astype(f32)
@@ -258,19 +313,24 @@
 
         high, low = split(later_in[h])
         leave = jnp.exp((group - offsets) * decay)
-        grad = g_ref[0, :, at]
-        value = moved[:, at]
-        wide = contract(mixing[h], grad, 0, 0) + leave * halves(
-            contract(k_ref[0, :, at], jnp.concatenate([high, low], axis=1), 1, 0)
+        table = jnp.where(between >= 0, jnp.exp(apart * decay), 0.0)
+        query, key = q_ref[0, :, at], k_ref[0, :, at]
+        grad, value = g_ref[0, :, at], moved[:, at]
+        mixing = (contract(query, key, 1, 1) * table).astype(bf16)
+        mixed = (contract(grad, value, 1, 1) * table).astype(bf16)
+        wide = contract(mixing, grad, 0, 0) + leave * halves(
+            contract(key, jnp.concatenate([high, low], axis=1), 1, 0)
         )
         grad_moved[:, at] = wide
-        picks[:npos, at] = contract(select, wide, 0, 0, highest)
-        mixed = (contract(grad, value, 1, 1) * table[h]).astype(bf16)
-        grad_mixing[h] = mixed
-        grad_key = contract(mixed, q_ref[0, :, at], 0, 0) + leave * halves(
+        picks[:npos, at] = halves(
+            contract(select_rows[...], jnp.concatenate(split(wide), axis=1), 1, 0)
+        )
+        grad_key = contract(mixed, query, 0, 0) + leave * halves(
             contract(value, jnp.concatenate([high, low], axis=0), 1, 1)
         )
         grad_key_ref[0, :, at] = grad_key.astype(bf16)
+        inner[:, at] = contract(mixing, value, 1, 0)
+        inner_query[:, at] = contract(mixed, key, 1, 0)
 
     def state_step(h):
         at = pl.ds(pl.multiple_of(h * size, size), size)
@@ -287,11 +347,11 @@
 
         high, low = split(state_in[h])
         enter = jnp.exp((offsets + 1.0) * decay)
-        attended = contract(mixing[h], moved[:, at], 1, 0) + enter * halves(
+        attended = inner[:, at] + enter * halves(
             contract(q_ref[0, :, at], jnp.concatenate([high, low], axis=1), 1, 0)
         )
         attended_ref[0, :, at] = attended.astype(bf16)
-        grad_query = contract(grad_mixing[h], k_ref[0, :, at], 1, 0) + enter * halves(
+        grad_query = inner_query[:, at] + enter * halves(
             contract(g_ref[0, :, at], jnp.concatenate([high, low], axis=0), 1, 1)
         )
         grad_query_ref[0, :, at] = grad_query.astype(bf16)
@@ -308,6 +368,8 @@
         return carry
 
     lax.fori_loop(0, heads, both_steps, 0)
+
+    stores[2].start()
 
     second[y] = jnp.zeros(second.shape[1:], f32)
     second[y, :, :npos] = contract(rows[...], picks[:npos, :], 1, 1, highest)
@@ -350,14 +412,14 @@
             - back_0 * refusal_ref[0:1, :]
             - back_1 * refusal_ref[1:2, :]
         )
-        bias_part = jnp.sum(code_grad, axis=1, keepdims=True)
+        bias_part = contract(jnp.ones((8, npos), f32), code_grad, 1, 1, highest)
         width = pay.shape[2]
         for owner in range(owners):
             at = slice(owner * width, (owner + 1) * width)
             pay[owner, 0:4, :] = rotation_part[:, at]
             pay[owner, 4:8, :] = weight_part[:, at]
-            pay[owner, 8:12, :] = jnp.broadcast_to(bias_part, (4, width))
-            pay[owner, 12:16, :] = jnp.zeros((4, width), f32)
+            pay[owner, 8:16, :] = jnp.zeros((8, width), f32)
+            pay[owner, 8:16, 0:4] = bias_part
 
             @pl.when(member == owner * stride)
             def _():
@@ -376,6 +438,7 @@
                     weight_ref[r : r + 1, at] - rows[r : r + 1, at]
                 )
             grad_value_ref[0, :, at] = wide.astype(bf16)
+        stores[3].start()
 
     along_own = along
 
@@ -388,6 +451,8 @@
         return carry
 
     lax.fori_loop(heads, heads + lag, rest, 0)
+    stores[0].start()
+    stores[1].start()
 
     @pl.when(z < last)
     def _():
@@ -451,9 +516,12 @@
         at = slice(owner * width, (owner + 1) * width)
         grad_rotation_ref[:, at] = total[owner, 0:4, :]
         grad_weight_ref[:, at] = total[owner, 4:8, :]
-    for r in range(4):
-        grad_bias_ref[r] = jnp.sum(total[0, 8 + r : 9 + r, 0:1])
-
+    grad_bias_ref[...] = total[0, 8:9, 0:4]
+    for i in range(4, 7):
+        stores[i].start()
+
+    for i in range(7):
+        stores[i].wait()
     for step in range(1, peers):
         across(first, first_send, first_recv, step).wait_send()
         across(second, second_send, second_recv, step).wait_send()
@@ -479,6 +547,17 @@
     @pl.when(owning)
     def _():
         lax.fori_loop(1, members, total_sent, 0)
+
+
+def store(*refs):
+    copies = [
+        pltpu.make_async_copy(source, target, refs[14].at[i])
+        for i, (source, target) in enumerate(zip(refs[:7], refs[7:14]))
+    ]
+    for copy in copies:
+        copy.start()
+    for copy in copies:
+        copy.wait()
 
 
 def shards(mesh, *arrays):
@@ -492,12 +571,12 @@
     npos = positions.shape[1]
     members = seqs * docs
     owners = min(members, width // 128)
-    vmem = pl.BlockSpec(memory_space=pltpu.VMEM)
-    smem = pl.BlockSpec(memory_space=pltpu.SMEM)
+    limit = 60 * 1024 * 1024
+    hbm = pl.BlockSpec(memory_space=pltpu.HBM)
     dma = pltpu.SemaphoreType.DMA
     square = (heads, size, size)
     big = jax.ShapeDtypeStruct(queries.shape, bf16)
-    return pl.pallas_call(
+    results = pl.pallas_call(
         functools.partial(kernel, (seqs, peers, docs, heads, owners)),
         out_shape=(
             big,
@@ -506,18 +585,37 @@
             big,
             jax.ShapeDtypeStruct(rotation.shape, f32),
             jax.ShapeDtypeStruct(weight.shape, f32),
-            jax.ShapeDtypeStruct(bias.shape, f32),
+            jax.ShapeDtypeStruct((1,) + bias.shape, f32),
         ),
-        in_specs=[vmem, vmem, vmem, vmem, smem, vmem, vmem, vmem, smem, vmem],
-        out_specs=(vmem, vmem, vmem, vmem, vmem, vmem, smem),
+        in_specs=[hbm] * 10,
+        out_specs=(hbm,) * 7,
         scratch_shapes=[
+            pltpu.VMEM(queries.shape, bf16),
+            pltpu.VMEM(queries.shape, bf16),
+            pltpu.VMEM(queries.shape, bf16),
+            pltpu.VMEM(queries.shape, bf16),
+            pltpu.VMEM(rotation.shape, f32),
+            pltpu.VMEM(weight.shape, f32),
+            pltpu.VMEM((1,) + bias.shape, f32),
+            dma((7,)),
+            pltpu.VMEM(queries.shape, bf16),
+            pltpu.VMEM(queries.shape, bf16),
+            pltpu.VMEM(queries.shape, bf16),
+            pltpu.VMEM(queries.shape, bf16),
+            pltpu.SMEM(decay_rate.shape, f32),
+            pltpu.VMEM(rotation.shape, f32),
+            pltpu.VMEM((2, width), f32),
+            pltpu.VMEM(weight.shape, f32),
+            pltpu.SMEM(bias.shape, f32),
+            pltpu.VMEM(positions.shape, jnp.int32),
+            dma((10,)),
+            pltpu.VMEM((npos, group), bf16),
+            pltpu.VMEM((group, width), f32),
+            pltpu.VMEM((group, width), f32),
             pltpu.VMEM((npos + 16, width), f32),
             pltpu.VMEM((npos, width), f32),
             pltpu.VMEM((8, width), f32),
             pltpu.VMEM((group, width), bf16),
-            pltpu.VMEM((heads, group, group), f32),
-            pltpu.VMEM((heads, group, group), bf16),
-            pltpu.VMEM((heads, group, group), bf16),
             pltpu.VMEM((group, width), f32),
             pltpu.VMEM(square, f32),
             pltpu.VMEM(square, f32),
@@ -542,9 +640,18 @@
             dma((owners,)),
         ],
         compiler_params=pltpu.CompilerParams(
-            collective_id=0, has_side_effects=True, vmem_limit_bytes=40 * 1024 * 1024
+            collective_id=0, has_side_effects=True, vmem_limit_bytes=limit
         ),
     )(queries, key_rows, values, out_grad, decay_rate, rotation, refusal.T, weight, bias, positions)
+    results = pl.pallas_call(
+        store,
+        out_shape=tuple(jax.ShapeDtypeStruct(x.shape, x.dtype) for x in results),
+        in_specs=[hbm] * 7,
+        out_specs=(hbm,) * 7,
+        scratch_shapes=[dma((7,))],
+        compiler_params=pltpu.CompilerParams(vmem_limit_bytes=limit),
+    )(*results)
+    return results[:6] + (results[6].reshape(bias.shape),)
 
 
 def solution(mesh):

time: 53.9 us -> 76 us (1.41)
  Pallas kernels: 41.7 us -> 75.2 us
  local copies, waits for them, and re-layouts: 11.1 us -> 0 us
    pallas_call x0 -> x1, Pallas kernels: none -> 33.9 us  [shards(): pl.pallas_call(store, out_shape=tuple((jax.ShapeDtypeStruct(x.shape, x.dt...]
    unnamed x27 -> x0, local copies, waits for them, and re-layouts: 11.1 us -> none
where the time goes in v2:
time: 76 us; the launch traced here: 75.9 us
  Pallas kernels  75.2 us (99%)
    pallas_call x1, Pallas kernels, shards(): pl.pallas_call(functools.partial(kernel, (seqs, peers, docs, heads, owner...  41.3 us
    pallas_call x1, Pallas kernels, shards(): pl.pallas_call(store, out_shape=tuple((jax.ShapeDtypeStruct(x.shape, x.dt...  33.9 us

profile of v2, /device:TPU:0, one launch (start us, length us, event | category | flops | bytes accessed | tf_op | source)
XLA Modules:
  0.0 75.9 jit_solution(5836239882245897798)
XLA Ops:
  0.6 41.3 %shard_map.153 = (bf16[1,128,1024]{2,1,0:T(8,128)(2,1)}, bf16[1,128,1024]{2,1,0:T(8,128)(2,1)}, bf16[1,128,1024]{2,1,0:T(8,128)(2,1)}, bf16[1,128,1024]{2,1,0:T(...) custom-call(bf16[1,128,1024]{2,1,0:T(8,128)(2,1)} %q_in.1, bf16[1,128,1024]{2,1,0:T(8,128)(2,1)} %k_in.1, ...), custom_call_target="tpu_custom_call" | custom-call | tf_op jit(solution)/shard_map/pallas_call | solution.py:579
  41.9 33.9 %shard_map.154 = (bf16[1,128,1024]{2,1,0:T(8,128)(2,1)}, bf16[1,128,1024]{2,1,0:T(8,128)(2,1)}, bf16[1,128,1024]{2,1,0:T(8,128)(2,1)}, bf16[1,128,1024]{2,1,0:T(...) custom-call(bf16[1,128,1024]{2,1,0:T(8,128)(2,1)} %get-tuple-element.21.refs_0_, ...), custom_call_target="tpu_custom_call" | custom-call | tf_op jit(solution)/shard_map/pallas_call | solution.py:646

commit v3 on v2

--- a/solution.py
+++ b/solution.py
@@ -110,15 +110,15 @@
         pltpu.make_async_copy(source, target, load_sem.at[i])
         for i, (source, target) in enumerate(
             (
+                (decay_in, decay_ref),
+                (q_in, q_ref),
+                (g_in, g_ref),
                 (v_in, v_ref),
                 (positions_in, positions_ref),
                 (weight_in, weight_ref),
                 (rotation_in, rotation_ref),
                 (refusal_in, refusal_ref),
-                (decay_in, decay_ref),
                 (bias_in, bias_ref),
-                (q_in, q_ref),
-                (g_in, g_ref),
                 (k_in, k_ref),
             )
         )
@@ -157,7 +157,68 @@
 
     lax.fori_loop(1, members, greet, 0)
 
-    for load in loads[:5]:
+    def across(buffer, send, recv, step):
+        other = lax.rem(y + step, peers)
+        return pltpu.make_async_remote_copy(
+            src_ref=buffer.at[y],
+            dst_ref=buffer.at[y],
+            send_sem=send.at[step - 1],
+            recv_sem=recv.at[y],
+            device_id={"head": other},
+            device_id_type=MESH,
+        )
+
+    def arrived(buffer, send, recv, step):
+        other = lax.rem(y + step, peers)
+        pltpu.make_async_remote_copy(
+            src_ref=buffer.at[other],
+            dst_ref=buffer.at[other],
+            send_sem=send.at[step - 1],
+            recv_sem=recv.at[other],
+            device_id={"head": other},
+            device_id_type=MESH,
+        ).wait_recv()
+
+    def state_copy(h):
+        return pltpu.make_async_remote_copy(
+            src_ref=state.at[h],
+            dst_ref=state_in.at[h],
+            send_sem=state_send.at[h],
+            recv_sem=state_recv.at[h],
+            device_id={"seq": lax.rem(z + 1, seqs)},
+            device_id_type=MESH,
+        )
+
+    def later_copy(h):
+        return pltpu.make_async_remote_copy(
+            src_ref=later.at[h],
+            dst_ref=later_in.at[h],
+            send_sem=later_send.at[h],
+            recv_sem=later_recv.at[h],
+            device_id={"seq": lax.rem(z + seqs - 1, seqs)},
+            device_id_type=MESH,
+        )
+
+    offsets = lax.broadcasted_iota(jnp.int32, (group, size), 0).astype(f32)
+
+    def log_decay(h):
+        return jnp.log1p(-jnp.full((1, size), decay_ref[h], f32))
+
+    for load in loads[:3]:
+        load.wait()
+    for h in range(heads):
+        at = slice(h * size, (h + 1) * size)
+        weighted = g_ref[0, :, at].astype(f32) * jnp.exp(offsets * log_decay(h))
+        both = jnp.concatenate(split(weighted), axis=1)
+        later[h] = halves(contract(q_ref[0, :, at], both, 0, 0))
+        if h == 0:
+            pl.semaphore_wait(barrier, peers - 1 + members - 1)
+
+        @pl.when(z == last)
+        def _():
+            later_copy(h).start()
+
+    for load in loads[3:8]:
         load.wait()
     places = z * group + lax.broadcasted_iota(jnp.int32, (group, npos), 0)
     chosen = places == positions_ref[...]
@@ -172,69 +233,8 @@
     stack[npos + 8 : npos + 10, :] = refusal_ref[...]
     first[y] = jnp.zeros(first.shape[1:], f32)
     first[y, :, : stack.shape[0]] = contract(stack[npos:, :], stack[...], 1, 1, highest)
-    pl.semaphore_wait(barrier, peers - 1 + members - 1)
-
-    def across(buffer, send, recv, step):
-        other = lax.rem(y + step, peers)
-        return pltpu.make_async_remote_copy(
-            src_ref=buffer.at[y],
-            dst_ref=buffer.at[y],
-            send_sem=send.at[step - 1],
-            recv_sem=recv.at[y],
-            device_id={"head": other},
-            device_id_type=MESH,
-        )
-
-    def arrived(buffer, send, recv, step):
-        other = lax.rem(y + step, peers)
-        pltpu.make_async_remote_copy(
-            src_ref=buffer.at[other],
-            dst_ref=buffer.at[other],
-            send_sem=send.at[step - 1],
-            recv_sem=recv.at[other],
-            device_id={"head": other},
-            device_id_type=MESH,
-        ).wait_recv()
-
     for step in range(1, peers):
         across(first, first_send, first_recv, step).start()
-
-    def state_copy(h):
-        return pltpu.make_async_remote_copy(
-            src_ref=state.at[h],
-            dst_ref=state_in.at[h],
-            send_sem=state_send.at[h],
-            recv_sem=state_recv.at[h],
-            device_id={"seq": lax.rem(z + 1, seqs)},
-            device_id_type=MESH,
-        )
-
-    def later_copy(h):
-        return pltpu.make_async_remote_copy(
-            src_ref=later.at[h],
-            dst_ref=later_in.at[h],
-            send_sem=later_send.at[h],
-            recv_sem=later_recv.at[h],
-            device_id={"seq": lax.rem(z + seqs - 1, seqs)},
-            device_id_type=MESH,
-        )
-
-    offsets = lax.broadcasted_iota(jnp.int32, (group, size), 0).astype(f32)
-
-    def log_decay(h):
-        return jnp.log1p(-jnp.full((1, size), decay_ref[h], f32))
-
-    for load in loads[5:9]:
-        load.wait()
-    for h in range(heads):
-        at = slice(h * size, (h + 1) * size)
-        weighted = g_ref[0, :, at].astype(f32) * jnp.exp(offsets * log_decay(h))
-        both = jnp.concatenate(split(weighted), axis=1)
-        later[h] = halves(contract(q_ref[0, :, at], both, 0, 0))
-
-        @pl.when(z == last)
-        def _():
-            later_copy(h).start()
 
     @pl.when(z == last)
     def _():
@@ -249,6 +249,7 @@
     )
     apart = jnp.maximum(between, 0).astype(f32)
 
+    loads[8].wait()
     for step in range(1, peers):
         arrived(first, first_send, first_recv, step)
     summed = first[0]
@@ -282,6 +283,23 @@
     )
     spread = contract(select, code, 1, 1, highest)
     loads[9].wait()
+
+    def later_forward(h, carry):
+        @pl.when(z < last)
+        def _():
+            later_copy(h).wait_recv()
+
+        @pl.when(jnp.logical_and(z > 0, z < last))
+        def _():
+            later[h] = later[h] + jnp.exp(group * log_decay(h)) * later_in[h]
+            later_copy(h).start()
+
+        return carry
+
+    most = min(4, heads)
+    ahead_count = jnp.where(z < last, jnp.clip(most - 2 * (last - 1 - z), 0, most), 0)
+    soon = ahead_count // 2
+    lax.fori_loop(0, soon, later_forward, 0)
     for h in range(heads):
         at = slice(h * size, (h + 1) * size)
         value = v_ref[0, :, at].astype(f32)
@@ -298,18 +316,15 @@
         def _():
             state_copy(h).start()
 
+    lax.fori_loop(soon, ahead_count, later_forward, 0)
+
     def later_step(h):
         at = pl.ds(pl.multiple_of(h * size, size), size)
         decay = log_decay(h)
 
-        @pl.when(z < last)
-        def _():
-            later_copy(h).wait_recv()
-
-        @pl.when(jnp.logical_and(z > 0, z < last))
-        def _():
-            later[h] = later[h] + jnp.exp(group * decay) * later_in[h]
-            later_copy(h).start()
+        @pl.when(h + ahead_count < heads)
+        def _():
+            later_forward(jnp.minimum(h + ahead_count, heads - 1), 0)
 
         high, low = split(later_in[h])
         leave = jnp.exp((group - offsets) * decay)
@@ -356,7 +371,7 @@
         )
         grad_query_ref[0, :, at] = grad_query.astype(bf16)
 
-    lag = jnp.clip(2 * (2 * z - last) + 3, 0, heads)
+    lag = jnp.clip(2 * (2 * z - last) + 3, 1, heads)
 
     def both_steps(i, carry):
         later_step(i)
@@ -550,11 +565,13 @@
 
 
 def store(*refs):
-    copies = [
-        pltpu.make_async_copy(source, target, refs[14].at[i])
-        for i, (source, target) in enumerate(zip(refs[:7], refs[7:14]))
-    ]
-    for copy in copies:
+    sources, targets, held, sems = refs[:7], refs[7:14], refs[14:21], refs[21]
+    fetches = [pltpu.make_async_copy(sources[i], held[i], sems.at[0, i]) for i in range(7)]
+    copies = [pltpu.make_async_copy(held[i], targets[i], sems.at[1, i]) for i in range(7)]
+    for fetch in fetches:
+        fetch.start()
+    for fetch, copy in zip(fetches, copies):
+        fetch.wait()
         copy.start()
     for copy in copies:
         copy.wait()
@@ -648,7 +665,7 @@
         out_shape=tuple(jax.ShapeDtypeStruct(x.shape, x.dtype) for x in results),
         in_specs=[hbm] * 7,
         out_specs=(hbm,) * 7,
-        scratch_shapes=[dma((7,))],
+        scratch_shapes=[pltpu.VMEM(x.shape, x.dtype) for x in results] + [dma((2, 7))],
         compiler_params=pltpu.CompilerParams(vmem_limit_bytes=limit),
     )(*results)
     return results[:6] + (results[6].reshape(bias.shape),)

time: 76 us -> 44.8 us (0.59)
  Pallas kernels: 75.2 us -> 44 us
    pallas_call x1, Pallas kernels: 33.9 us -> 2.04 us  [shards(): pl.pallas_call(store, out_shape=tuple((jax.ShapeDtypeStruct(x.shape, x.dt...]
where the time goes in v3:
time: 44.8 us; the launch traced here: 44.6 us
  Pallas kernels  44 us (98%)
  between operations  0.64 us (1%)
    pallas_call x1, Pallas kernels, shards(): pl.pallas_call(functools.partial(kernel, (seqs, peers, docs, heads, owner...  41.9 us
    pallas_call x1, Pallas kernels, shards(): pl.pallas_call(store, out_shape=tuple((jax.ShapeDtypeStruct(x.shape, x.dt...  2.04 us

profile of v3, /device:TPU:0, one launch (start us, length us, event | category | flops | bytes accessed | tf_op | source)
XLA Modules:
  0.0 44.6 jit_solution(14561880937351171127)
XLA Ops:
  0.6 41.9 %shard_map.153 = (bf16[1,128,1024]{2,1,0:T(8,128)(2,1)}, bf16[1,128,1024]{2,1,0:T(8,128)(2,1)}, bf16[1,128,1024]{2,1,0:T(8,128)(2,1)}, bf16[1,128,1024]{2,1,0:T(...) custom-call(bf16[1,128,1024]{2,1,0:T(8,128)(2,1)} %q_in.1, bf16[1,128,1024]{2,1,0:T(8,128)(2,1)} %k_in.1, ...), custom_call_target="tpu_custom_call" | custom-call | tf_op jit(solution)/shard_map/pallas_call | solution.py:596
  42.6 2.0 %shard_map.154 = (bf16[1,128,1024]{2,1,0:T(8,128)(2,1)}, bf16[1,128,1024]{2,1,0:T(8,128)(2,1)}, bf16[1,128,1024]{2,1,0:T(8,128)(2,1)}, bf16[1,128,1024]{2,1,0:T(...) custom-call(bf16[1,128,1024]{2,1,0:T(8,128)(2,1)} %get-tuple-element.21.refs_0_, ...), custom_call_target="tpu_custom_call" | custom-call | tf_op jit(solution)/shard_map/pallas_call | solution.py:663

commit v4 on v3

--- a/solution.py
+++ b/solution.py
@@ -69,6 +69,7 @@
     select_rows,
     inner,
     inner_query,
+    inner_key,
     stack,
     picks,
     rows,
@@ -110,14 +111,14 @@
         pltpu.make_async_copy(source, target, load_sem.at[i])
         for i, (source, target) in enumerate(
             (
-                (decay_in, decay_ref),
-                (q_in, q_ref),
-                (g_in, g_ref),
                 (v_in, v_ref),
                 (positions_in, positions_ref),
                 (weight_in, weight_ref),
                 (rotation_in, rotation_ref),
                 (refusal_in, refusal_ref),
+                (q_in, q_ref),
+                (g_in, g_ref),
+                (decay_in, decay_ref),
                 (bias_in, bias_ref),
                 (k_in, k_ref),
             )
@@ -204,21 +205,7 @@
     def log_decay(h):
         return jnp.log1p(-jnp.full((1, size), decay_ref[h], f32))
 
-    for load in loads[:3]:
-        load.wait()
-    for h in range(heads):
-        at = slice(h * size, (h + 1) * size)
-        weighted = g_ref[0, :, at].astype(f32) * jnp.exp(offsets * log_decay(h))
-        both = jnp.concatenate(split(weighted), axis=1)
-        later[h] = halves(contract(q_ref[0, :, at], both, 0, 0))
-        if h == 0:
-            pl.semaphore_wait(barrier, peers - 1 + members - 1)
-
-        @pl.when(z == last)
-        def _():
-            later_copy(h).start()
-
-    for load in loads[3:8]:
+    for load in loads[:5]:
         load.wait()
     places = z * group + lax.broadcasted_iota(jnp.int32, (group, npos), 0)
     chosen = places == positions_ref[...]
@@ -233,8 +220,32 @@
     stack[npos + 8 : npos + 10, :] = refusal_ref[...]
     first[y] = jnp.zeros(first.shape[1:], f32)
     first[y, :, : stack.shape[0]] = contract(stack[npos:, :], stack[...], 1, 1, highest)
+    pl.semaphore_wait(barrier, peers - 1 + members - 1)
     for step in range(1, peers):
         across(first, first_send, first_recv, step).start()
+
+    for load in loads[5:8]:
+        load.wait()
+
+    def own_later(h):
+        at = slice(h * size, (h + 1) * size)
+        weighted = g_ref[0, :, at].astype(f32) * jnp.exp(offsets * log_decay(h))
+        both = jnp.concatenate(split(weighted), axis=1)
+        later[h] = halves(contract(q_ref[0, :, at], both, 0, 0))
+
+    own_later(0)
+
+    @pl.when(z == last)
+    def _():
+        later_copy(0).start()
+
+    for h in range(1, heads):
+        own_later(h)
+
+    @pl.when(z == last)
+    def _():
+        for h in range(1, heads):
+            later_copy(h).start()
 
     @pl.when(z == last)
     def _():
@@ -296,11 +307,19 @@
 
         return carry
 
-    most = min(4, heads)
-    ahead_count = jnp.where(z < last, jnp.clip(most - 2 * (last - 1 - z), 0, most), 0)
-    soon = ahead_count // 2
-    lax.fori_loop(0, soon, later_forward, 0)
-    for h in range(heads):
+    def state_forward(h, carry):
+        @pl.when(z > 0)
+        def _():
+            state_copy(h).wait_recv()
+
+        @pl.when(jnp.logical_and(z > 0, z < last))
+        def _():
+            state[h] = state[h] + jnp.exp(group * log_decay(h)) * state_in[h]
+            state_copy(h).start()
+
+        return carry
+
+    def own_state(h):
         at = slice(h * size, (h + 1) * size)
         value = v_ref[0, :, at].astype(f32)
         shift = spread[:, 0:1] * rows[0:1, at]
@@ -312,56 +331,67 @@
         both = jnp.concatenate(split(weighted), axis=1)
         state[h] = halves(contract(k_ref[0, :, at], both, 0, 0))
 
-        @pl.when(z == 0)
-        def _():
+    own_state(0)
+
+    @pl.when(z == 0)
+    def _():
+        state_copy(0).start()
+
+    for h in range(1, heads):
+        own_state(h)
+
+    @pl.when(z == 0)
+    def _():
+        for h in range(1, heads):
             state_copy(h).start()
 
-    lax.fori_loop(soon, ahead_count, later_forward, 0)
-
-    def later_step(h):
-        at = pl.ds(pl.multiple_of(h * size, size), size)
-        decay = log_decay(h)
-
-        @pl.when(h + ahead_count < heads)
-        def _():
-            later_forward(jnp.minimum(h + ahead_count, heads - 1), 0)
-
-        high, low = split(later_in[h])
-        leave = jnp.exp((group - offsets) * decay)
-        table = jnp.where(between >= 0, jnp.exp(apart * decay), 0.0)
+    def local(h):
+        at = slice(h * size, (h + 1) * size)
+        table = jnp.where(between >= 0, jnp.exp(apart * log_decay(h)), 0.0)
         query, key = q_ref[0, :, at], k_ref[0, :, at]
         grad, value = g_ref[0, :, at], moved[:, at]
         mixing = (contract(query, key, 1, 1) * table).astype(bf16)
         mixed = (contract(grad, value, 1, 1) * table).astype(bf16)
-        wide = contract(mixing, grad, 0, 0) + leave * halves(
-            contract(key, jnp.concatenate([high, low], axis=1), 1, 0)
+        grad_moved[:, at] = contract(mixing, grad, 0, 0)
+        inner_key[:, at] = contract(mixed, query, 0, 0)
+        inner[:, at] = contract(mixing, value, 1, 0)
+        inner_query[:, at] = contract(mixed, key, 1, 0)
+
+    near = z == last - 1
+    half = heads // 2
+    one = jnp.where(near, min(1, heads), 0)
+    two = jnp.where(near, min(2, heads), 0)
+    ahead = jnp.where(near, min(3, heads), jnp.where(z == last - 2, min(1, heads), 0))
+    state_ahead = jnp.where(jnp.logical_and(z == 1, z < last), min(1, heads), 0)
+    lax.fori_loop(0, one, later_forward, 0)
+    for h in range(half):
+        local(h)
+    lax.fori_loop(one, two, later_forward, 0)
+    for h in range(half, heads):
+        local(h)
+    lax.fori_loop(two, ahead, later_forward, 0)
+    lax.fori_loop(0, state_ahead, state_forward, 0)
+
+    def later_outer(h):
+        at = pl.ds(pl.multiple_of(h * size, size), size)
+        high, low = split(later_in[h])
+        leave = jnp.exp((group - offsets) * log_decay(h))
+        wide = grad_moved[:, at] + leave * halves(
+            contract(k_ref[0, :, at], jnp.concatenate([high, low], axis=1), 1, 0)
         )
         grad_moved[:, at] = wide
         picks[:npos, at] = halves(
             contract(select_rows[...], jnp.concatenate(split(wide), axis=1), 1, 0)
         )
-        grad_key = contract(mixed, query, 0, 0) + leave * halves(
-            contract(value, jnp.concatenate([high, low], axis=0), 1, 1)
+        grad_key = inner_key[:, at] + leave * halves(
+            contract(moved[:, at], jnp.concatenate([high, low], axis=0), 1, 1)
         )
         grad_key_ref[0, :, at] = grad_key.astype(bf16)
-        inner[:, at] = contract(mixing, value, 1, 0)
-        inner_query[:, at] = contract(mixed, key, 1, 0)
-
-    def state_step(h):
+
+    def state_outer(h):
         at = pl.ds(pl.multiple_of(h * size, size), size)
-        decay = log_decay(h)
-
-        @pl.when(z > 0)
-        def _():
-            state_copy(h).wait_recv()
-
-        @pl.when(jnp.logical_and(z > 0, z < last))
-        def _():
-            state[h] = state[h] + jnp.exp(group * decay) * state_in[h]
-            state_copy(h).start()
-
         high, low = split(state_in[h])
-        enter = jnp.exp((offsets + 1.0) * decay)
+        enter = jnp.exp((offsets + 1.0) * log_decay(h))
         attended = inner[:, at] + enter * halves(
             contract(q_ref[0, :, at], jnp.concatenate([high, low], axis=1), 1, 0)
         )
@@ -371,18 +401,27 @@
         )
         grad_query_ref[0, :, at] = grad_query.astype(bf16)
 
-    lag = jnp.clip(2 * (2 * z - last) + 3, 1, heads)
-
-    def both_steps(i, carry):
-        later_step(i)
-
-        @pl.when(i >= lag)
-        def _():
-            state_step(jnp.maximum(i - lag, 0))
-
-        return carry
-
-    lax.fori_loop(0, heads, both_steps, 0)
+    @pl.when(z == last)
+    def _():
+        for h in range(heads):
+            later_outer(h)
+
+    @pl.when(z < last)
+    def _():
+        def both_steps(i, carry):
+            @pl.when(i + ahead < heads)
+            def _():
+                later_forward(jnp.minimum(i + ahead, heads - 1), 0)
+
+            @pl.when(i + state_ahead < heads)
+            def _():
+                state_forward(jnp.minimum(i + state_ahead, heads - 1), 0)
+
+            later_outer(i)
+            state_outer(i)
+            return carry
+
+        lax.fori_loop(0, heads, both_steps, 0)
 
     stores[2].start()
 
@@ -461,11 +500,15 @@
     def _():
         finish_code()
 
-    def rest(i, carry):
-        state_step(i - lag)
-        return carry
-
-    lax.fori_loop(heads, heads + lag, rest, 0)
+    @pl.when(z == last)
+    def _():
+        def rest(i, carry):
+            state_forward(i, 0)
+            state_outer(i)
+            return carry
+
+        lax.fori_loop(0, heads, rest, 0)
+
     stores[0].start()
     stores[1].start()
 
@@ -629,6 +672,7 @@
             pltpu.VMEM((npos, group), bf16),
             pltpu.VMEM((group, width), f32),
             pltpu.VMEM((group, width), f32),
+            pltpu.VMEM((group, width), f32),
             pltpu.VMEM((npos + 16, width), f32),
             pltpu.VMEM((npos, width), f32),
             pltpu.VMEM((8, width), f32),

time: 44.8 us -> 44.2 us (0.987)
  Pallas kernels: 44 us -> 43.4 us
    pallas_call x1, Pallas kernels: 41.9 us -> 41.3 us  [shards(): pl.pallas_call(functools.partial(kernel, (seqs, peers, docs, heads, owner...]
where the time goes in v4:
time: 44.2 us; the launch traced here: 44 us
  Pallas kernels  43.4 us (98%)
  between operations  0.64 us (1%)
    pallas_call x1, Pallas kernels, shards(): pl.pallas_call(functools.partial(kernel, (seqs, peers, docs, heads, owner...  41.3 us
    pallas_call x1, Pallas kernels, shards(): pl.pallas_call(store, out_shape=tuple((jax.ShapeDtypeStruct(x.shape, x.dt...  2.04 us

profile of v4, /device:TPU:0, one launch (start us, length us, event | category | flops | bytes accessed | tf_op | source)
XLA Modules:
  0.0 44.0 jit_solution(4624379476330727082)
XLA Ops:
  0.6 41.3 %shard_map.153 = (bf16[1,128,1024]{2,1,0:T(8,128)(2,1)}, bf16[1,128,1024]{2,1,0:T(8,128)(2,1)}, bf16[1,128,1024]{2,1,0:T(8,128)(2,1)}, bf16[1,128,1024]{2,1,0:T(...) custom-call(bf16[1,128,1024]{2,1,0:T(8,128)(2,1)} %q_in.1, bf16[1,128,1024]{2,1,0:T(8,128)(2,1)} %k_in.1, ...), custom_call_target="tpu_custom_call" | custom-call | tf_op jit(solution)/shard_map/pallas_call | solution.py:639
  42.0 2.0 %shard_map.154 = (bf16[1,128,1024]{2,1,0:T(8,128)(2,1)}, bf16[1,128,1024]{2,1,0:T(8,128)(2,1)}, bf16[1,128,1024]{2,1,0:T(8,128)(2,1)}, bf16[1,128,1024]{2,1,0:T(...) custom-call(bf16[1,128,1024]{2,1,0:T(8,128)(2,1)} %get-tuple-element.21.refs_0_, ...), custom_call_target="tpu_custom_call" | custom-call | tf_op jit(solution)/shard_map/pallas_call | solution.py:707

commit v5 on v4

--- a/solution.py
+++ b/solution.py
@@ -10,6 +10,7 @@
 MESH = pl.DeviceIdType.MESH
 f32 = jnp.float32
 bf16 = jnp.bfloat16
+PIECES = 4
 
 
 def contract(a, b, da, db, precision=None):
@@ -180,22 +181,32 @@
             device_id_type=MESH,
         ).wait_recv()
 
-    def state_copy(h):
+    depth = size // PIECES
+    pieces = heads * PIECES
+
+    def piece(n):
+        if isinstance(n, int):
+            return n // PIECES, slice(n % PIECES * depth, (n % PIECES + 1) * depth)
+        return n // PIECES, pl.ds(pl.multiple_of(lax.rem(n, PIECES) * depth, depth), depth)
+
+    def state_copy(n):
+        h, at = piece(n)
         return pltpu.make_async_remote_copy(
-            src_ref=state.at[h],
-            dst_ref=state_in.at[h],
-            send_sem=state_send.at[h],
-            recv_sem=state_recv.at[h],
+            src_ref=state.at[h, at],
+            dst_ref=state_in.at[h, at],
+            send_sem=state_send.at[n],
+            recv_sem=state_recv.at[n],
             device_id={"seq": lax.rem(z + 1, seqs)},
             device_id_type=MESH,
         )
 
-    def later_copy(h):
+    def later_copy(n):
+        h, at = piece(n)
         return pltpu.make_async_remote_copy(
-            src_ref=later.at[h],
-            dst_ref=later_in.at[h],
-            send_sem=later_send.at[h],
-            recv_sem=later_recv.at[h],
+            src_ref=later.at[h, at],
+            dst_ref=later_in.at[h, at],
+            send_sem=later_send.at[n],
+            recv_sem=later_recv.at[n],
             device_id={"seq": lax.rem(z + seqs - 1, seqs)},
             device_id_type=MESH,
         )
@@ -237,15 +248,16 @@
 
     @pl.when(z == last)
     def _():
-        later_copy(0).start()
+        for n in range(PIECES):
+            later_copy(n).start()
 
     for h in range(1, heads):
         own_later(h)
 
     @pl.when(z == last)
     def _():
-        for h in range(1, heads):
-            later_copy(h).start()
+        for n in range(PIECES, pieces):
+            later_copy(n).start()
 
     @pl.when(z == last)
     def _():
@@ -295,27 +307,31 @@
     spread = contract(select, code, 1, 1, highest)
     loads[9].wait()
 
-    def later_forward(h, carry):
+    def later_forward(n, carry):
+        h, at = piece(n)
+
         @pl.when(z < last)
         def _():
-            later_copy(h).wait_recv()
+            later_copy(n).wait_recv()
 
         @pl.when(jnp.logical_and(z > 0, z < last))
         def _():
-            later[h] = later[h] + jnp.exp(group * log_decay(h)) * later_in[h]
-            later_copy(h).start()
+            later[h, at] = later[h, at] + jnp.exp(group * log_decay(h)) * later_in[h, at]
+            later_copy(n).start()
 
         return carry
 
-    def state_forward(h, carry):
+    def state_forward(n, carry):
+        h, at = piece(n)
+
         @pl.when(z > 0)
         def _():
-            state_copy(h).wait_recv()
+            state_copy(n).wait_recv()
 
         @pl.when(jnp.logical_and(z > 0, z < last))
         def _():
-            state[h] = state[h] + jnp.exp(group * log_decay(h)) * state_in[h]
-            state_copy(h).start()
+            state[h, at] = state[h, at] + jnp.exp(group * log_decay(h)) * state_in[h, at]
+            state_copy(n).start()
 
         return carry
 
@@ -335,15 +351,16 @@
 
     @pl.when(z == 0)
     def _():
-        state_copy(0).start()
+        for n in range(PIECES):
+            state_copy(n).start()
 
     for h in range(1, heads):
         own_state(h)
 
     @pl.when(z == 0)
     def _():
-        for h in range(1, heads):
-            state_copy(h).start()
+        for n in range(PIECES, pieces):
+            state_copy(n).start()
 
     def local(h):
         at = slice(h * size, (h + 1) * size)
@@ -358,19 +375,21 @@
         inner_query[:, at] = contract(mixed, key, 1, 0)
 
     near = z == last - 1
-    half = heads // 2
-    one = jnp.where(near, min(1, heads), 0)
-    two = jnp.where(near, min(2, heads), 0)
-    ahead = jnp.where(near, min(3, heads), jnp.where(z == last - 2, min(1, heads), 0))
-    state_ahead = jnp.where(jnp.logical_and(z == 1, z < last), min(1, heads), 0)
-    lax.fori_loop(0, one, later_forward, 0)
-    for h in range(half):
-        local(h)
-    lax.fori_loop(one, two, later_forward, 0)
-    for h in range(half, heads):
-        local(h)
-    lax.fori_loop(two, ahead, later_forward, 0)
-    lax.fori_loop(0, state_ahead, state_forward, 0)
+    far = jnp.logical_and(z == 1, z < last - 1)
+    blocks = 4
+    later_plan = (3, 4, 5, 6, 6)
+    state_plan = (0, 0, 1, 2, 2)
+    laters, states = 0, 0
+    for block in range(blocks + 1):
+        for h in range((block - 1) * heads // blocks, block * heads // blocks):
+            if block > 0:
+                local(h)
+        goal = jnp.where(near, min(later_plan[block], pieces), 0)
+        lax.fori_loop(laters, goal, later_forward, 0)
+        laters = goal
+        goal = jnp.where(far, min(state_plan[block], pieces), 0)
+        lax.fori_loop(states, goal, state_forward, 0)
+        states = goal
 
     def later_outer(h):
         at = pl.ds(pl.multiple_of(h * size, size), size)
@@ -408,20 +427,23 @@
 
     @pl.when(z < last)
     def _():
-        def both_steps(i, carry):
-            @pl.when(i + ahead < heads)
+        def both_steps(n, carry):
+            @pl.when(n + laters < pieces)
             def _():
-                later_forward(jnp.minimum(i + ahead, heads - 1), 0)
-
-            @pl.when(i + state_ahead < heads)
+                later_forward(jnp.minimum(n + laters, pieces - 1), 0)
+
+            @pl.when(n + states < pieces)
             def _():
-                state_forward(jnp.minimum(i + state_ahead, heads - 1), 0)
-
-            later_outer(i)
-            state_outer(i)
+                state_forward(jnp.minimum(n + states, pieces - 1), 0)
+
+            @pl.when(lax.rem(n, PIECES) == PIECES - 1)
+            def _():
+                later_outer(n // PIECES)
+                state_outer(n // PIECES)
+
             return carry
 
-        lax.fori_loop(0, heads, both_steps, 0)
+        lax.fori_loop(0, pieces, both_steps, 0)
 
     stores[2].start()
 
@@ -503,7 +525,8 @@
     @pl.when(z == last)
     def _():
         def rest(i, carry):
-            state_forward(i, 0)
+            for p in range(PIECES):
+                state_forward(i * PIECES + p, 0)
             state_outer(i)
             return carry
 
@@ -584,18 +607,18 @@
         across(first, first_send, first_recv, step).wait_send()
         across(second, second_send, second_recv, step).wait_send()
 
-    def sent(h, carry):
+    def sent(n, carry):
         @pl.when(z < last)
         def _():
-            state_copy(h).wait_send()
+            state_copy(n).wait_send()
 
         @pl.when(z > 0)
         def _():
-            later_copy(h).wait_send()
+            later_copy(n).wait_send()
 
         return carry
 
-    lax.fori_loop(0, heads, sent, 0)
+    lax.fori_loop(0, pieces, sent, 0)
     for owner in range(owners):
 
         @pl.when(member != owner * stride)
@@ -691,10 +714,10 @@
             dma((peers,)),
             dma((peers,)),
             dma((peers,)),
-            dma((heads,)),
-            dma((heads,)),
-            dma((heads,)),
-            dma((heads,)),
+            dma((heads * PIECES,)),
+            dma((heads * PIECES,)),
+            dma((heads * PIECES,)),
+            dma((heads * PIECES,)),
             dma((owners,)),
             dma((members,)),
             dma((members,)),

time: 44.2 us -> 52.5 us (1.19)
  Pallas kernels: 43.4 us -> 51.7 us
    pallas_call x1, Pallas kernels: 41.3 us -> 49.7 us  [shards(): pl.pallas_call(functools.partial(kernel, (seqs, peers, docs, heads, owner...]
where the time goes in v5:
time: 52.5 us; the launch traced here: 52.3 us
  Pallas kernels  51.7 us (98%)
  between operations  0.64 us (1%)
    pallas_call x1, Pallas kernels, shards(): pl.pallas_call(functools.partial(kernel, (seqs, peers, docs, heads, owner...  49.7 us
    pallas_call x1, Pallas kernels, shards(): pl.pallas_call(store, out_shape=tuple((jax.ShapeDtypeStruct(x.shape, x.dt...  2.04 us

profile of v5, /device:TPU:0, one launch (start us, length us, event | category | flops | bytes accessed | tf_op | source)
XLA Modules:
  0.0 52.3 jit_solution(18300433887785915936)
XLA Ops:
  0.6 49.7 %shard_map.153 = (bf16[1,128,1024]{2,1,0:T(8,128)(2,1)}, bf16[1,128,1024]{2,1,0:T(8,128)(2,1)}, bf16[1,128,1024]{2,1,0:T(8,128)(2,1)}, bf16[1,128,1024]{2,1,0:T(...) custom-call(bf16[1,128,1024]{2,1,0:T(8,128)(2,1)} %q_in.1, bf16[1,128,1024]{2,1,0:T(8,128)(2,1)} %k_in.1, ...), custom_call_target="tpu_custom_call" | custom-call | tf_op jit(solution)/shard_map/pallas_call | solution.py:662
  50.3 2.0 %shard_map.154 = (bf16[1,128,1024]{2,1,0:T(8,128)(2,1)}, bf16[1,128,1024]{2,1,0:T(8,128)(2,1)}, bf16[1,128,1024]{2,1,0:T(8,128)(2,1)}, bf16[1,128,1024]{2,1,0:T(...) custom-call(bf16[1,128,1024]{2,1,0:T(8,128)(2,1)} %get-tuple-element.21.refs_0_, ...), custom_call_target="tpu_custom_call" | custom-call | tf_op jit(solution)/shard_map/pallas_call | solution.py:730

commit v6 on v4

--- a/solution.py
+++ b/solution.py
@@ -361,16 +361,16 @@
     half = heads // 2
     one = jnp.where(near, min(1, heads), 0)
     two = jnp.where(near, min(2, heads), 0)
-    ahead = jnp.where(near, min(3, heads), jnp.where(z == last - 2, min(1, heads), 0))
-    state_ahead = jnp.where(jnp.logical_and(z == 1, z < last), min(1, heads), 0)
+    ahead = jnp.where(near, min(4, heads), 0)
+    state_ahead = jnp.where(jnp.logical_and(z == 1, z < last - 1), min(1, heads), 0)
     lax.fori_loop(0, one, later_forward, 0)
     for h in range(half):
         local(h)
     lax.fori_loop(one, two, later_forward, 0)
+    lax.fori_loop(0, state_ahead, state_forward, 0)
     for h in range(half, heads):
         local(h)
     lax.fori_loop(two, ahead, later_forward, 0)
-    lax.fori_loop(0, state_ahead, state_forward, 0)
 
     def later_outer(h):
         at = pl.ds(pl.multiple_of(h * size, size), size)

time: 44.2 us -> 42.8 us (0.968)
  Pallas kernels: 43.4 us -> 42 us
    pallas_call x1, Pallas kernels: 41.3 us -> 39.9 us  [shards(): pl.pallas_call(functools.partial(kernel, (seqs, peers, docs, heads, owner...]
where the time goes in v6:
time: 42.8 us; the launch traced here: 42.6 us
  Pallas kernels  42 us (98%)
  between operations  0.64 us (1%)
    pallas_call x1, Pallas kernels, shards(): pl.pallas_call(functools.partial(kernel, (seqs, peers, docs, heads, owner...  39.9 us
    pallas_call x1, Pallas kernels, shards(): pl.pallas_call(store, out_shape=tuple((jax.ShapeDtypeStruct(x.shape, x.dt...  2.04 us

profile of v6, /device:TPU:0, one launch (start us, length us, event | category | flops | bytes accessed | tf_op | source)
XLA Modules:
  0.0 42.6 jit_solution(6048441063354758402)
XLA Ops:
  0.6 39.9 %shard_map.153 = (bf16[1,128,1024]{2,1,0:T(8,128)(2,1)}, bf16[1,128,1024]{2,1,0:T(8,128)(2,1)}, bf16[1,128,1024]{2,1,0:T(8,128)(2,1)}, bf16[1,128,1024]{2,1,0:T(...) custom-call(bf16[1,128,1024]{2,1,0:T(8,128)(2,1)} %q_in.1, bf16[1,128,1024]{2,1,0:T(8,128)(2,1)} %k_in.1, ...), custom_call_target="tpu_custom_call" | custom-call | tf_op jit(solution)/shard_map/pallas_call | solution.py:639
  40.6 2.0 %shard_map.154 = (bf16[1,128,1024]{2,1,0:T(8,128)(2,1)}, bf16[1,128,1024]{2,1,0:T(8,128)(2,1)}, bf16[1,128,1024]{2,1,0:T(8,128)(2,1)}, bf16[1,128,1024]{2,1,0:T(...) custom-call(bf16[1,128,1024]{2,1,0:T(8,128)(2,1)} %get-tuple-element.21.refs_0_, ...), custom_call_target="tpu_custom_call" | custom-call | tf_op jit(solution)/shard_map/pallas_call | solution.py:707

commit v7 on v6

--- a/solution.py
+++ b/solution.py
@@ -67,6 +67,7 @@
     positions_ref,
     load_sem,
     select_rows,
+    chosen_rows,
     inner,
     inner_query,
     inner_key,
@@ -205,27 +206,26 @@
     def log_decay(h):
         return jnp.log1p(-jnp.full((1, size), decay_ref[h], f32))
 
-    for load in loads[:5]:
-        load.wait()
-    places = z * group + lax.broadcasted_iota(jnp.int32, (group, npos), 0)
-    chosen = places == positions_ref[...]
-    select = jnp.where(chosen, 1.0, 0.0)
-    turned = select.T
-    select_rows[...] = turned.astype(bf16)
-    stack[npos:, :] = jnp.zeros((stack.shape[0] - npos, stack.shape[1]), f32)
-    picked = contract(select_rows[...], v_ref[0], 1, 0)
-    stack[:npos, :] = picked
-    stack[npos : npos + 4, :] = weight_ref[...]
-    stack[npos + 4 : npos + 8, :] = rotation_ref[...]
-    stack[npos + 8 : npos + 10, :] = refusal_ref[...]
-    first[y] = jnp.zeros(first.shape[1:], f32)
-    first[y, :, : stack.shape[0]] = contract(stack[npos:, :], stack[...], 1, 1, highest)
-    pl.semaphore_wait(barrier, peers - 1 + members - 1)
-    for step in range(1, peers):
-        across(first, first_send, first_recv, step).start()
-
-    for load in loads[5:8]:
-        load.wait()
+    def project(ready):
+        for load in loads[:5]:
+            load.wait()
+        places = z * group + lax.broadcasted_iota(jnp.int32, (group, npos), 0)
+        chosen = places == positions_ref[...]
+        chosen_rows[...] = jnp.where(chosen, 1.0, 0.0)
+        turned = chosen_rows[...].T
+        select_rows[...] = turned.astype(bf16)
+        stack[npos:, :] = jnp.zeros((stack.shape[0] - npos, stack.shape[1]), f32)
+        picked = contract(select_rows[...], v_ref[0], 1, 0)
+        stack[:npos, :] = picked
+        stack[npos : npos + 4, :] = weight_ref[...]
+        stack[npos + 4 : npos + 8, :] = rotation_ref[...]
+        stack[npos + 8 : npos + 10, :] = refusal_ref[...]
+        first[y] = jnp.zeros(first.shape[1:], f32)
+        first[y, :, : stack.shape[0]] = contract(stack[npos:, :], stack[...], 1, 1, highest)
+        if not ready:
+            pl.semaphore_wait(barrier, peers - 1 + members - 1)
+        for step in range(1, peers):
+            across(first, first_send, first_recv, step).start()
 
     def own_later(h):
         at = slice(h * size, (h + 1) * size)
@@ -233,19 +233,30 @@
         both = jnp.concatenate(split(weighted), axis=1)
         later[h] = halves(contract(q_ref[0, :, at], both, 0, 0))
 
-    own_later(0)
+    def own_laters():
+        for load in loads[5:8]:
+            load.wait()
+        own_later(0)
+        for h in range(1, heads):
+            own_later(h)
 
     @pl.when(z == last)
     def _():
+        for load in loads[5:8]:
+            load.wait()
+        own_later(0)
+        pl.semaphore_wait(barrier, peers - 1 + members - 1)
         later_copy(0).start()
-
-    for h in range(1, heads):
-        own_later(h)
-
-    @pl.when(z == last)
-    def _():
+        for h in range(1, heads):
+            own_later(h)
         for h in range(1, heads):
             later_copy(h).start()
+        project(True)
+
+    @pl.when(z < last)
+    def _():
+        project(False)
+        own_laters()
 
     @pl.when(z == last)
     def _():
@@ -292,7 +303,7 @@
         + bias
         - (summed[4:8, :npos] - map_0 * along[0:1, :] - map_1 * along[1:2, :])
     )
-    spread = contract(select, code, 1, 1, highest)
+    spread = contract(chosen_rows[...], code, 1, 1, highest)
     loads[9].wait()
 
     def later_forward(h, carry):
@@ -337,6 +348,10 @@
     def _():
         state_copy(0).start()
 
+    near = z == last - 1
+    mid = jnp.logical_and(z == last - 2, z > 0)
+    one = jnp.where(near, min(1, heads), 0)
+    lax.fori_loop(0, one, later_forward, 0)
     for h in range(1, heads):
         own_state(h)
 
@@ -357,20 +372,19 @@
         inner[:, at] = contract(mixing, value, 1, 0)
         inner_query[:, at] = contract(mixed, key, 1, 0)
 
-    near = z == last - 1
     half = heads // 2
-    one = jnp.where(near, min(1, heads), 0)
     two = jnp.where(near, min(2, heads), 0)
-    ahead = jnp.where(near, min(4, heads), 0)
+    three = jnp.where(near, min(3, heads), jnp.where(mid, min(1, heads), 0))
+    ahead = jnp.where(near, min(4, heads), jnp.where(mid, min(1, heads), 0))
     state_ahead = jnp.where(jnp.logical_and(z == 1, z < last - 1), min(1, heads), 0)
-    lax.fori_loop(0, one, later_forward, 0)
+    lax.fori_loop(one, two, later_forward, 0)
     for h in range(half):
         local(h)
-    lax.fori_loop(one, two, later_forward, 0)
+    lax.fori_loop(two, three, later_forward, 0)
     lax.fori_loop(0, state_ahead, state_forward, 0)
     for h in range(half, heads):
         local(h)
-    lax.fori_loop(two, ahead, later_forward, 0)
+    lax.fori_loop(three, ahead, later_forward, 0)
 
     def later_outer(h):
         at = pl.ds(pl.multiple_of(h * size, size), size)
@@ -442,6 +456,7 @@
         )
 
     def finish_code():
+        forth = contract(code, picks[:npos, :], 1, 0, highest)
         for step in range(1, peers):
             arrived(second, second_send, second_recv, step)
         sums = second[0]
@@ -461,7 +476,7 @@
         back_1 = projected[0] * inverse[0][1] + projected[1] * inverse[1][1]
         weight_part = contract(code_grad, stack[:npos, :], 1, 0, highest)
         rotation_part = (
-            contract(code, picks[:npos, :], 1, 0, highest)
+            forth
             - weight_part
             - back_0 * refusal_ref[0:1, :]
             - back_1 * refusal_ref[1:2, :]
@@ -483,7 +498,7 @@
             def _():
                 part_copy(owner).start()
 
-        spread_grad = contract(select, code_grad, 1, 1, highest)
+        spread_grad = contract(chosen_rows[...], code_grad, 1, 1, highest)
         for h in range(heads):
             at = slice(h * size, (h + 1) * size)
             wide = grad_moved[:, at]
@@ -670,6 +685,7 @@
             pltpu.VMEM(positions.shape, jnp.int32),
             dma((10,)),
             pltpu.VMEM((npos, group), bf16),
+            pltpu.VMEM((group, npos), f32),
             pltpu.VMEM((group, width), f32),
             pltpu.VMEM((group, width), f32),
             pltpu.VMEM((group, width), f32),

time: 42.8 us -> 42.8 us (level)
  no operation moved by 1% of the time
where the time goes in v7:
time: 42.8 us; the launch traced here: 42.6 us
  Pallas kernels  42 us (98%)
  between operations  0.64 us (1%)
    pallas_call x1, Pallas kernels, shards(): pl.pallas_call(functools.partial(kernel, (seqs, peers, docs, heads, owner...  39.9 us
    pallas_call x1, Pallas kernels, shards(): pl.pallas_call(store, out_shape=tuple((jax.ShapeDtypeStruct(x.shape, x.dt...  2.04 us

profile of v7, /device:TPU:0, one launch (start us, length us, event | category | flops | bytes accessed | tf_op | source)
XLA Modules:
  0.0 42.6 jit_solution(898901560461551899)
XLA Ops:
  0.6 39.9 %shard_map.153 = (bf16[1,128,1024]{2,1,0:T(8,128)(2,1)}, bf16[1,128,1024]{2,1,0:T(8,128)(2,1)}, bf16[1,128,1024]{2,1,0:T(8,128)(2,1)}, bf16[1,128,1024]{2,1,0:T(...) custom-call(bf16[1,128,1024]{2,1,0:T(8,128)(2,1)} %q_in.1, bf16[1,128,1024]{2,1,0:T(8,128)(2,1)} %k_in.1, ...), custom_call_target="tpu_custom_call" | custom-call | tf_op jit(solution)/shard_map/pallas_call | solution.py:654
  40.6 2.0 %shard_map.154 = (bf16[1,128,1024]{2,1,0:T(8,128)(2,1)}, bf16[1,128,1024]{2,1,0:T(8,128)(2,1)}, bf16[1,128,1024]{2,1,0:T(8,128)(2,1)}, bf16[1,128,1024]{2,1,0:T(...) custom-call(bf16[1,128,1024]{2,1,0:T(8,128)(2,1)} %get-tuple-element.21.refs_0_, ...), custom_call_target="tpu_custom_call" | custom-call | tf_op jit(solution)/shard_map/pallas_call | solution.py:723

commit v8 on v7

--- a/solution.py
+++ b/solution.py
@@ -375,16 +375,19 @@
     half = heads // 2
     two = jnp.where(near, min(2, heads), 0)
     three = jnp.where(near, min(3, heads), jnp.where(mid, min(1, heads), 0))
-    ahead = jnp.where(near, min(4, heads), jnp.where(mid, min(1, heads), 0))
-    state_ahead = jnp.where(jnp.logical_and(z == 1, z < last - 1), min(1, heads), 0)
+    ahead = jnp.where(near, min(5, heads), jnp.where(mid, min(1, heads), 0))
+    far = jnp.logical_and(z == 1, z < last - 1)
+    state_one = jnp.where(far, min(1, heads), 0)
+    state_ahead = jnp.where(far, min(2, heads), 0)
     lax.fori_loop(one, two, later_forward, 0)
     for h in range(half):
         local(h)
     lax.fori_loop(two, three, later_forward, 0)
-    lax.fori_loop(0, state_ahead, state_forward, 0)
+    lax.fori_loop(0, state_one, state_forward, 0)
     for h in range(half, heads):
         local(h)
     lax.fori_loop(three, ahead, later_forward, 0)
+    lax.fori_loop(state_one, state_ahead, state_forward, 0)
 
     def later_outer(h):
         at = pl.ds(pl.multiple_of(h * size, size), size)

time: 42.8 us -> 42.2 us (0.986)
  Pallas kernels: 42 us -> 41.4 us
    pallas_call x1, Pallas kernels: 39.9 us -> 39.3 us  [shards(): pl.pallas_call(functools.partial(kernel, (seqs, peers, docs, heads, owner...]
where the time goes in v8:
time: 42.2 us; the launch traced here: 42 us
  Pallas kernels  41.4 us (98%)
  between operations  0.64 us (2%)
    pallas_call x1, Pallas kernels, shards(): pl.pallas_call(functools.partial(kernel, (seqs, peers, docs, heads, owner...  39.3 us
    pallas_call x1, Pallas kernels, shards(): pl.pallas_call(store, out_shape=tuple((jax.ShapeDtypeStruct(x.shape, x.dt...  2.04 us

profile of v8, /device:TPU:0, one launch (start us, length us, event | category | flops | bytes accessed | tf_op | source)
XLA Modules:
  0.0 42.0 jit_solution(15069930128906980344)
XLA Ops:
  0.6 39.3 %shard_map.153 = (bf16[1,128,1024]{2,1,0:T(8,128)(2,1)}, bf16[1,128,1024]{2,1,0:T(8,128)(2,1)}, bf16[1,128,1024]{2,1,0:T(8,128)(2,1)}, bf16[1,128,1024]{2,1,0:T(...) custom-call(bf16[1,128,1024]{2,1,0:T(8,128)(2,1)} %q_in.1, bf16[1,128,1024]{2,1,0:T(8,128)(2,1)} %k_in.1, ...), custom_call_target="tpu_custom_call" | custom-call | tf_op jit(solution)/shard_map/pallas_call | solution.py:657
  40.0 2.0 %shard_map.154 = (bf16[1,128,1024]{2,1,0:T(8,128)(2,1)}, bf16[1,128,1024]{2,1,0:T(8,128)(2,1)}, bf16[1,128,1024]{2,1,0:T(8,128)(2,1)}, bf16[1,128,1024]{2,1,0:T(...) custom-call(bf16[1,128,1024]{2,1,0:T(8,128)(2,1)} %get-tuple-element.21.refs_0_, ...), custom_call_target="tpu_custom_call" | custom-call | tf_op jit(solution)/shard_map/pallas_call | solution.py:726
